TPU v7x, 32 devices: a whole 2x2x4 slice. The times are simulated.
32 devices in a mesh: head: 4 (over y, x), node: 8 (over z, core).
Axes of the slice: x: 2, y: 2, z: 4, core: 2. Of those that a mesh axis runs over, the one named last changes fastest.
Arguments:
- prev_state: float32 [98304, 84], P('node'), may hold values from -6 to 6
- target: float32 [98304, 84], P('node')
- noise_eps: float32 [98304, 84], P('node'), may hold values from -6 to 6
- noise_level: int32 [1], replicated, may hold values from 0 to 999
- valid_count: int32 [8], P('node'), may hold values from 1 to 2048, as said below
- neighbours: int32 [16384, 16], P('node'), may hold values from 0 to 16383, as said below
- nbr_count: int32 [16384], P('node'), may hold values from 8 to 16
- pix_node: int32 [98304], P('node'), may hold values from 0 to 16383, as said below
- pix_read: int32 [98304, 3], P('node'), may hold values from 0 to 16383, as said below
- w_enc: float32 [168, 512], replicated, may hold values from -0.1875 to 0.1875
- w_cond: float32 [32, 2048], replicated, may hold values from -1 to 1
- w_dec: float32 [512, 84], replicated, may hold values from -0.25 to 0.25
- layer_w: float32 [3, 512, 2048], P(None, 'node', 'head'), may hold values from -0.25 to 0.25
- soap_first: float32 [3, 512, 2048], P(None, 'node', 'head'), may hold values from -9.536743e-06 to 9.536743e-06
- soap_second: float32 [3, 512, 2048], P(None, 'node', 'head'), may hold values from 1.57566e-12 to 6.30264e-12
- soap_basis: float32 [3, 4, 512, 512], P(None, 'head')
- soap_stats: float32 [3, 4, 512, 512], P(None, 'head')
- enc_first: float32 [168, 512], replicated, may hold values from -9.536743e-06 to 9.536743e-06
- enc_second: float32 [168, 512], replicated, may hold values from 1.57566e-12 to 6.30264e-12
- cond_first: float32 [32, 2048], replicated, may hold values from -9.536743e-06 to 9.536743e-06
- cond_second: float32 [32, 2048], replicated, may hold values from 1.57566e-12 to 6.30264e-12
- dec_first: float32 [512, 84], replicated, may hold values from -9.536743e-06 to 9.536743e-06
- dec_second: float32 [512, 84], replicated, may hold values from 1.57566e-12 to 6.30264e-12
Outputs:
- loss_sum: float32 [1], replicated
- loss_count: float32 [1], replicated
- grad_norm: float32 [1], replicated
- layer_w_new: float32 [3, 512, 2048], P(None, 'node', 'head')
- soap_first_new: float32 [3, 512, 2048], P(None, 'node', 'head')
- soap_second_new: float32 [3, 512, 2048], P(None, 'node', 'head')
- soap_basis_new: float32 [3, 4, 512, 512], P(None, 'head')
- soap_stats_new: float32 [3, 4, 512, 512], P(None, 'head')
- w_enc_new: float32 [168, 512], replicated
- enc_first_new: float32 [168, 512], replicated
- enc_second_new: float32 [168, 512], replicated
- w_cond_new: float32 [32, 2048], replicated
- cond_first_new: float32 [32, 2048], replicated
- cond_second_new: float32 [32, 2048], replicated
- w_dec_new: float32 [512, 84], replicated
- dec_first_new: float32 [512, 84], replicated
- dec_second_new: float32 [512, 84], replicated
Inputs may be any that keep to these rules, and one draw needn't show every extreme that they name: `pix_node`: pixel p encodes into a node of block p // 12288 of 2048 nodes. `pix_read`: pixel p reads three nodes of block p // 12288. The neighbours of a node of block b lie in blocks b - 1, b and b + 1 of 2048 nodes, cyclically. `valid_count`: the last block's nodes are all valid.
All inputs are finite; a program needn't handle non-finite values.
Results may differ from a plain program's by a relative error of at most 0.0074.
Values may be sent and summed in bfloat16 or wider, within the bound.
A program may use at most 320 MiB of HBM per device.

v0:
```python
import functools
import math

import jax
import jax.numpy as jnp
from jax import lax
from jax.experimental import pallas as pl
from jax.experimental.pallas import tpu as pltpu
from jax.sharding import PartitionSpec as P

HD = 128
VARS = 84
NF = 32
NBR = 16
LEVELS = 1000
STEP = 10

SLOT = 128
SLIM = 96
GROUP = 256 // NBR
BLOCK = 128
STRIP = 16
HEAD_STEP = 17

highest = lax.Precision.HIGHEST
clip_limit = 0.01
beta_first = 0.9
beta_second = 0.95
beta_stats = 0.95
adam_epsilon = 1e-08
rate_layer = 0.02
rate_small = 0.05
decay_rate = 0.1
norm_eps = 1e-05

f32 = jnp.float32
bf16 = jnp.bfloat16
MIB = 2**20


def passed_along(x, axis, by):
    length = lax.axis_size(axis)
    return lax.ppermute(x, axis, [(i, (i + by) % length) for i in range(length)])


def noise_terms(noise_level):
    level_frac = noise_level[0].astype(f32) / (LEVELS - 1)
    noise_sigma = 0.05 * jnp.exp(level_frac * math.log(40.0))
    frequency = 1.0 + jnp.arange(NF // 2).astype(f32)
    phase_angle = jnp.log(noise_sigma) * frequency
    return (noise_sigma, jnp.concatenate([jnp.sin(phase_angle), jnp.cos(phase_angle)]))


def standardize(values_in):
    row_mean = jnp.mean(values_in, -1, keepdims=True)
    centered = values_in - row_mean
    inv_std = lax.rsqrt(jnp.mean(centered * centered, -1, keepdims=True) + norm_eps)
    return (centered * inv_std, inv_std)


def norm_back(normed, inv_std, grad_in):
    return inv_std * (
        grad_in
        - jnp.mean(grad_in, -1, keepdims=True)
        - normed * jnp.mean(grad_in * normed, -1, keepdims=True)
    )


def contract(left, right, left_dim, right_dim, precision=None):
    return lax.dot_general(
        left,
        right,
        (((left_dim,), (right_dim,)), ((), ())),
        preferred_element_type=f32,
        precision=precision,
    )


def halves(x):
    high = x.astype(bf16)
    return high, (x - high.astype(f32)).astype(bf16)


def thirds(x):
    high = x.astype(bf16)
    rest = x - high.astype(f32)
    return (high, *halves(rest))


def fold_lanes(x, op=jnp.add):
    parts = [x[:, i : i + 128] for i in range(0, x.shape[1], 128)]
    while len(parts) > 1:
        parts = [op(*parts[i : i + 2]) if i + 1 < len(parts) else parts[i] for i in range(0, len(parts), 2)]
    return parts[0]


def adam_small(weight, grad_item, first, second):
    first_new = beta_first * first + (1 - beta_first) * grad_item
    second_new = beta_second * second + (1 - beta_second) * grad_item * grad_item
    ratio = (
        first_new
        / (1 - beta_first**STEP)
        / (jnp.sqrt(second_new / (1 - beta_second**STEP)) + adam_epsilon)
    )
    return (weight - rate_small * (ratio + decay_rate * weight), first_new, second_new)


def smem():
    return pl.BlockSpec(memory_space=pltpu.SMEM)


def whole(shape):
    zeros = (0,) * len(shape)
    return pl.BlockSpec(tuple(shape), lambda *_: zeros)


def params(mib=48):
    return pltpu.CompilerParams(vmem_limit_bytes=mib * MIB)


def remote(mib, identity):
    return pltpu.CompilerParams(
        vmem_limit_bytes=mib * MIB, collective_id=identity, has_side_effects=True
    )


def vmem():
    return pl.BlockSpec(memory_space=pltpu.VMEM)


def hbm():
    return pl.BlockSpec(memory_space=pl.ANY)


def each(count, act, start=1):
    def body(off, carry):
        act(off)
        return carry

    lax.fori_loop(start, count, body, 0)


def meet(axes):
    barrier = pltpu.get_barrier_semaphore()
    total = 0
    for axis in axes:
        count, me = lax.axis_size(axis), lax.axis_index(axis)
        total += count - 1
        each(
            count,
            lambda off: pl.semaphore_signal(barrier, inc=1, device_id={axis: (me + off) % count}),
        )
    pl.semaphore_wait(barrier, total)


class Spread:
    def __init__(self, group, source, target, sends, receives):
        self.count, self.me, self.where = group
        self.source, self.target = source, target
        self.sends, self.receives = sends, receives

    def copy(self, other, slot):
        return pltpu.make_async_remote_copy(
            src_ref=self.source(other),
            dst_ref=self.target(slot),
            send_sem=self.sends.at[other],
            recv_sem=self.receives.at[slot],
            device_id=self.where(other),
        )

    def other(self, off):
        return (self.me + off) % self.count

    def start(self, off):
        self.copy(self.other(off), self.me).start()

    def arrived(self, off):
        self.copy(self.other(off), self.other(off)).wait_recv()

    def sent(self, off):
        self.copy(self.other(off), self.me).wait_send()

    def all(self, act):
        each(self.count, getattr(self, act))


def along(axis):
    return lax.axis_size(axis), lax.axis_index(axis), lambda other: {axis: other}


def pairs():
    node = lax.axis_index("node")
    place, pair = node % 2, node // 2
    within = (2, place, lambda other: {"node": 2 * pair + other})
    across = (lax.axis_size("node") // 2, pair, lambda other: {"node": 2 * other + place})
    return within, across


def encode_kernel(
    place_ref, scale_ref, node_ref, prev_ref, target_ref, eps_ref, w_ref, in_ref, stat_ref, own_ref, all_ref,
    pix, box, pair_box, sems, pair_sems
):
    step = pl.program_id(0)
    rows = in_ref.shape[0]
    tile = node_ref.shape[1]
    within, across = pairs()
    place = within[1]
    weights = Spread(across, lambda _: w_ref, lambda i: box.at[i], sems.at[0], sems.at[1])
    swap = pltpu.make_async_remote_copy(
        src_ref=box,
        dst_ref=pair_box,
        send_sem=pair_sems.at[0],
        recv_sem=pair_sems.at[1],
        device_id=within[2](1 - place),
    )

    @pl.when(step == 0)
    def _():
        meet(["node"])
        weights.all("start")
        box[weights.me] = w_ref[...]
        pix[...] = jnp.zeros_like(pix)
        in_ref[...] = jnp.zeros_like(in_ref)
        stat_ref[...] = jnp.zeros_like(stat_ref)

    @pl.when(step == pl.num_programs(0) - 2)
    def _():
        weights.all("arrived")
        swap.start()

    prev = prev_ref[...]
    target = target_ref[...]
    noisy = target + scale_ref[0] * eps_ref[...]
    pix[:VARS] = prev.astype(bf16)
    pix[SLOT : SLOT + VARS] = (scale_ref[1] * noisy).astype(bf16)
    node = node_ref[...] - place_ref[0]
    mine = node - place_ref[1]
    spot = lax.broadcasted_iota(jnp.int32, (rows, tile), 0)
    onehot = (spot == mine).astype(f32).astype(bf16)
    in_ref[...] += contract(onehot, pix[...], 1, 1)
    valid = (node < place_ref[2]).astype(f32)
    residual = target - prev
    stat_ref[:VARS] += fold_lanes(valid * residual * residual)
    stat_ref[SLIM - 1 : SLIM] += fold_lanes(valid)

    @pl.when(step == pl.num_programs(0) - 1)
    def _():
        swap.wait()
        own_ref[...] = box[...]
        all_ref[:, place] = box[...]
        all_ref[:, 1 - place] = pair_box[...]
        weights.all("sent")


def encode(place, scales, node_row, prev, target, eps, w_share, rows, tile, nodes):
    pixels = prev.shape[1]
    column = (nodes // 2, *w_share.shape)
    gathered = (nodes // 2, 2, *w_share.shape)
    pixel_block = pl.BlockSpec((VARS, tile), lambda i: (0, i))
    return pl.pallas_call(
        encode_kernel,
        grid=(pixels // tile,),
        in_specs=[smem(), smem(), pl.BlockSpec((1, tile), lambda i: (0, i))]
        + [pixel_block] * 3
        + [whole(w_share.shape)],
        out_specs=[whole((rows, 2 * SLOT)), whole((SLIM, 128)), whole(column), whole(gathered)],
        out_shape=[
            jax.ShapeDtypeStruct((rows, 2 * SLOT), f32),
            jax.ShapeDtypeStruct((SLIM, 128), f32),
            jax.ShapeDtypeStruct(column, bf16),
            jax.ShapeDtypeStruct(gathered, bf16),
        ],
        scratch_shapes=[
            pltpu.VMEM((2 * SLOT, tile), bf16),
            pltpu.VMEM(column, bf16),
            pltpu.VMEM(column, bf16),
            pltpu.SemaphoreType.DMA((2, nodes // 2)),
            pltpu.SemaphoreType.DMA((2,)),
        ],
        compiler_params=remote(48, 2),
        name="encode",
    )(place, scales, node_row, prev, target, eps, w_share)


def count_tile(band_rows, spot_rows, put, bands):
    lane = lax.broadcasted_iota(jnp.int32, (GROUP, 256), 1)
    sub = lax.broadcasted_iota(jnp.int32, (GROUP, 256), 0)
    own = lane % GROUP == sub
    widen = (lane // GROUP == sub).astype(f32).astype(bf16)
    all_bands = contract(band_rows, widen, 0, 0)
    all_spots = contract(spot_rows, widen, 0, 0)
    spot = lax.broadcasted_iota(jnp.int32, (256, 256), 0).astype(f32)
    for g in range(band_rows.shape[1] // GROUP):
        nodes = slice(g * GROUP, (g + 1) * GROUP)
        band = jnp.where(own, all_bands[nodes], -1.0)
        left = jnp.concatenate([(band == t).astype(f32).astype(bf16) for t in range(bands)], 0)
        row = jnp.sum(jnp.where(own, all_spots[nodes], 0.0), 0, keepdims=True)
        right = (spot == row).astype(f32).astype(bf16)
        found = contract(left, right, 1, 1).astype(bf16)
        for t in range(bands):
            put(g, t, found[t * GROUP : (t + 1) * GROUP])


def nearest_first(me, count):
    if count == 4:
        return [me + 1 - 2 * (me % 2), (me + 2) % 4, 3 - me]
    return [(me + k) % count for k in range(1, count)]


def open_kernel(
    in_ref, wenc_ref, mod_ref, stat_ref, w_ref, nbr_ref, live_ref,
    zero_ref, norm_ref, q_ref, kv_ref, sum_ref, count_ref,
    stat_own, stat_box, bands, spots, tiles, head_sems, stat_sems, halo_sems, out_sems,
):
    heads, rows, _ = norm_ref.shape
    head, node = lax.axis_index("head"), lax.axis_index("node")
    groups = lax.axis_size("node")
    depth = tiles.shape[1]
    nodes = count_ref.shape[0]
    steps = nodes // depth
    stat_own[...] = jnp.broadcast_to(jnp.sum(stat_ref[...], 1, keepdims=True), stat_own.shape)
    meet(["head", "node"])

    stats = Spread(along("node"), lambda _: stat_own, lambda i: stat_box.at[i], stat_sems.at[0], stat_sems.at[1])
    stats.all("start")
    w_enc = wenc_ref[...]
    h_zero = sum(contract(part, w_enc, 1, 0) for part in thirds(in_ref[...]))
    zero_ref[...] = h_zero
    normed, _ = standardize(h_zero)
    norm_ref[head] = (normed * (1 + mod_ref[0:1]) + mod_ref[1:2]).astype(bf16)
    norms = Spread(
        along("head"), lambda _: norm_ref.at[head], lambda i: norm_ref.at[i], head_sems.at[0], head_sems.at[1]
    )
    near = nearest_first(head, heads)
    for other in near[:2]:
        norms.copy(other, head).start()

    def halo(block):
        return [
            pltpu.make_async_remote_copy(
                src_ref=kv_ref.at[1, block],
                dst_ref=kv_ref.at[2 * side, block],
                send_sem=halo_sems.at[2 * side, block],
                recv_sem=halo_sems.at[2 * side + 1, block],
                device_id={"node": (node + by) % groups},
            )
            for side, by in enumerate((1, groups - 1))
        ]

    def project(block):
        out = contract(norm_ref[block], w_ref[:, : 3 * HD], 1, 0).astype(bf16)
        q_ref[block] = out[:, :HD]
        kv_ref[1, block] = out[:, HD:]
        for copy in halo(block):
            copy.start()

    def count(step):
        slot = step % 2

        @pl.when(step >= 2)
        def _():
            count_out(step - 2).wait()

        here = pl.ds(pl.multiple_of(step * depth, depth), depth)

        def put(g, t, found):
            tiles[slot, g * GROUP : (g + 1) * GROUP, t * 256 : (t + 1) * 256] = found

        count_tile(bands[:, here], spots[:, here], put, tiles.shape[2] // 256)
        count_out(step).start()

    def count_out(step):
        return pltpu.make_async_copy(
            tiles.at[step % 2],
            count_ref.at[pl.ds(pl.multiple_of(step * depth, depth), depth)],
            out_sems.at[step % 2],
        )

    project(head)
    total = nodes * groups
    relative = nbr_ref[...] - node * nodes + nodes
    relative = jnp.where(relative >= total, relative - total, relative)
    relative = jnp.where(relative < 0, relative + total, relative)
    live = lax.broadcasted_iota(jnp.int32, relative.shape, 0) < live_ref[...]
    bands[...] = jnp.where(live, relative >> 8, -1).astype(f32).astype(bf16)
    spots[...] = (relative & 255).astype(f32).astype(bf16)
    each(steps // 4, count, 0)

    norms.copy(near[0], near[0]).wait_recv()
    for other in near[2:]:
        norms.copy(other, head).start()
    project(near[0])
    norms.copy(near[1], near[1]).wait_recv()
    project(near[1])
    each(steps * 5 // 8, count, steps // 4)
    for other in near[2:]:
        norms.copy(other, other).wait_recv()
        project(other)
    each(steps, count, steps * 5 // 8)
    each(steps, lambda step: count_out(step).wait(), steps - 2)
    stats.all("arrived")
    sum_ref[...] = sum(jnp.where(t == node, stat_own[...], stat_box[t]) for t in range(groups))

    def finish(block):
        for copy in halo(block):
            copy.wait()

    each(heads, finish, 0)
    norms.all("sent")
    stats.all("sent")


def open_nodes(node_in, w_enc, modulation, stat, w_attn, neighbours, live, heads, groups):
    rows, width = node_in.shape[0], w_enc.shape[1]
    depth = 8 * GROUP
    reach = 3 * heads * rows
    block = lambda w: jax.ShapeDtypeStruct((heads, rows, w), bf16)
    return pl.pallas_call(
        open_kernel,
        in_specs=[vmem()] * 7,
        out_specs=[vmem()] * 5 + [pl.BlockSpec(memory_space=pl.ANY)],
        out_shape=[
            jax.ShapeDtypeStruct((rows, width), f32),
            block(width),
            block(HD),
            jax.ShapeDtypeStruct((3, heads, rows, 2 * HD), bf16),
            jax.ShapeDtypeStruct((SLIM, 128), f32),
            jax.ShapeDtypeStruct((heads * rows, reach), bf16),
        ],
        scratch_shapes=[
            pltpu.VMEM((SLIM, 128), f32),
            pltpu.VMEM((groups, SLIM, 128), f32),
            pltpu.VMEM((NBR, heads * rows), bf16),
            pltpu.VMEM((NBR, heads * rows), bf16),
            pltpu.VMEM((2, depth, reach), bf16),
            pltpu.SemaphoreType.DMA((2, heads)),
            pltpu.SemaphoreType.DMA((2, groups)),
            pltpu.SemaphoreType.DMA((4, heads)),
            pltpu.SemaphoreType.DMA((2,)),
        ],
        compiler_params=remote(56, 3),
        name="open_nodes",
    )(node_in, w_enc, modulation, stat, w_attn, neighbours, live)


def attend_kernel(
    q_ref, kv_ref, count_ref, column_ref, ffn_ref, e_ref, mix_ref, out_ref, attn_all, ffn_all, s_scr, own, box, sems,
    attn_sems, column_sems, ffn_sems, pair_sems, local_sems, chunk
):
    step = pl.program_id(0)
    steps = pl.num_programs(0)
    head = lax.axis_index("head")
    tile = q_ref.shape[0]
    per = box.shape[1] // tile

    def copy(target, source, part):
        at = pl.ds(pl.multiple_of(part * tile, tile), tile)
        return pltpu.make_async_remote_copy(
            src_ref=own.at[target, at],
            dst_ref=box.at[source, at],
            send_sem=sems.at[0, target, part],
            recv_sem=sems.at[1, source, part],
            device_id={"head": target},
        )

    within, across = pairs()
    place, pair = within[1], across[1]
    attn_heads = Spread(
        along("head"), lambda _: column_ref, lambda i: attn_all.at[i, :, place], attn_sems.at[0], attn_sems.at[1]
    )
    ffn_pairs = Spread(
        across, lambda _: ffn_ref, lambda i: ffn_all.at[head, i, place], column_sems.at[0], column_sems.at[1]
    )
    ffn_heads = Spread(
        along("head"),
        lambda _: ffn_all.at[head, :, place],
        lambda i: ffn_all.at[i, :, place],
        ffn_sems.at[0],
        ffn_sems.at[1],
    )
    stay = [
        pltpu.make_async_copy(column_ref, attn_all.at[head, :, place], local_sems.at[0]),
        pltpu.make_async_copy(ffn_ref, ffn_all.at[head, pair, place], local_sems.at[1]),
    ]

    def swap(h, which, side):
        array = (attn_all, ffn_all)[which]
        return pltpu.make_async_remote_copy(
            src_ref=array.at[h, :, side],
            dst_ref=array.at[h, :, side],
            send_sem=pair_sems.at[0, which, h],
            recv_sem=pair_sems.at[1, which, h],
            device_id=within[2](1 - place),
        )

    @pl.when(step == 0)
    def _():
        meet(["head", "node"])
        ffn_pairs.all("start")
        attn_heads.all("start")
        for copy in stay:
            copy.start()

    @pl.when(step == steps * 5 // 16)
    def _():
        ffn_pairs.all("arrived")
        for copy in stay:
            copy.wait()
        ffn_heads.all("start")

    @pl.when(step == steps * 14 // 16)
    def _():
        attn_heads.all("arrived")
        ffn_heads.all("arrived")

        def begin(h):
            for which in range(2):
                swap(h, which, place).start()

        each(box.shape[0], begin, 0)

    nodes = kv_ref.shape[1]
    q = q_ref[...]
    top = jnp.full((tile, 128), -1e30, f32)
    for b in range(3):
        for at in range(0, nodes, chunk):
            cols = slice(b * nodes + at, b * nodes + at + chunk)
            s = contract(q, kv_ref[b, at : at + chunk, :HD], 1, 1)
            s = jnp.where(count_ref[:, cols].astype(f32) > 0, s, -1e30)
            s_scr[:, cols] = s
            top = jnp.maximum(top, fold_lanes(s, jnp.maximum))
    top = jnp.max(top, 1, keepdims=True)
    factor = math.log2(math.e) / math.sqrt(HD)
    total = jnp.zeros((tile, 128), f32)
    mixed = jnp.zeros((tile, HD), f32)
    for b in range(3):
        for at in range(0, nodes, chunk):
            cols = slice(b * nodes + at, b * nodes + at + chunk)
            e = count_ref[:, cols].astype(f32) * jnp.exp2((s_scr[:, cols] - top) * factor)
            total += fold_lanes(e)
            e = e.astype(bf16)
            e_ref[:, cols] = e
            mixed += contract(e, kv_ref[b, at : at + chunk, HD:], 1, 0)
    inverse = 1.0 / jnp.sum(total, 1, keepdims=True)
    mixed = mixed * inverse
    mix_ref[:, :HD] = mixed
    mix_ref[:, HD:] = jnp.broadcast_to(inverse, (tile, HD))
    target, part = step // per, step % per
    at = pl.ds(pl.multiple_of(part * tile, tile), tile)
    low = mixed.astype(bf16)
    own[target, at] = low

    @pl.when(target == head)
    def _():
        box[head, at] = low

    @pl.when(target != head)
    def _():
        copy(target, head, part).start()

    @pl.when(step == steps - 1)
    def _():
        heads = box.shape[0]

        def finish(off):
            other = (head + off) % heads
            for p in range(per):
                copy(other, other, p).wait_recv()
                copy(other, head, p).wait_send()

        each(heads, finish)
        out_ref[...] = box[...]

        def end(h):
            for which in range(2):
                swap(h, which, place).wait_send()
                swap(h, which, 1 - place).wait_recv()

        each(heads, end, 0)
        for spread in (attn_heads, ffn_pairs, ffn_heads):
            spread.all("sent")


def attend(query, keyval, counts, column, ffn_share, heads, tile, chunk):
    nodes, reach = counts.shape
    rows = nodes // heads
    count = column.shape[0]
    dma = lambda *shape: pltpu.SemaphoreType.DMA(shape)
    row = lambda width: pl.BlockSpec((tile, width), lambda i: (i, 0))
    return pl.pallas_call(
        functools.partial(attend_kernel, chunk=chunk),
        grid=(nodes // tile,),
        in_specs=[row(HD), whole(keyval.shape), row(reach), hbm(), hbm()],
        out_specs=[row(reach), row(2 * HD), whole((heads, rows, HD)), hbm(), hbm()],
        out_shape=[
            jax.ShapeDtypeStruct((nodes, reach), bf16),
            jax.ShapeDtypeStruct((nodes, 2 * HD), f32),
            jax.ShapeDtypeStruct((heads, rows, HD), bf16),
            jax.ShapeDtypeStruct((heads, count, 2, *column.shape[1:]), bf16),
            jax.ShapeDtypeStruct((heads, count, 2, *ffn_share.shape), bf16),
        ],
        scratch_shapes=[
            pltpu.VMEM((tile, reach), f32),
            pltpu.VMEM((heads, rows, HD), bf16),
            pltpu.VMEM((heads, rows, HD), bf16),
            dma(2, heads, rows // tile),
            dma(2, heads),
            dma(2, count),
            dma(2, heads),
            dma(2, 2, heads),
            dma(2),
        ],
        compiler_params=remote(60, 4),
        name="attend",
    )(query, keyval, counts, column, ffn_share)


def attend_back_kernel(
    q_ref, d_ref, mix_ref, e_ref, kv_ref, norm_ref, pair_sum,
    dq_ref, dkv_ref, grad_ref, share_ref, full_ref,
    dk, dv, dq, low_own, high_own, low_box, high_box, dq_own, dq_box, dkv_own, dkv_box,
    head_box, across_own, across_box, share_low, full,
    halo_sems, dq_sems, dkv_sems, pair_sems, head_sems, across_sems, full_sems,
    chunk,
):
    turn, part = pl.program_id(0), pl.program_id(1)
    parts = pl.num_programs(1)
    step = turn * parts + part
    tile = q_ref.shape[0]
    nodes = kv_ref.shape[1]
    heads, rows, _ = dq_box.shape
    per = rows // tile
    head, node, groups = lax.axis_index("head"), lax.axis_index("node"), lax.axis_size("node")
    within, across = pairs()
    last = part == parts - 1

    place, pair = within[1], across[1]
    over_heads = Spread(
        along("head"), lambda o: pair_sum.at[o], lambda i: head_box.at[i], head_sems.at[0], head_sems.at[1]
    )
    over_pairs = Spread(
        across, lambda o: across_own.at[o], lambda i: across_box.at[i], across_sems.at[0], across_sems.at[1]
    )
    over_full = Spread(
        across, lambda _: share_low, lambda i: full.at[place, i], full_sems.at[0], full_sems.at[1]
    )
    count = across[0]

    def swap(side):
        return pltpu.make_async_remote_copy(
            src_ref=full.at[side],
            dst_ref=full.at[side],
            send_sem=pair_sems.at[0],
            recv_sem=pair_sems.at[1],
            device_id=within[2](1 - place),
        )

    def halo(own, box, side, by):
        return pltpu.make_async_remote_copy(
            src_ref=own,
            dst_ref=box,
            send_sem=halo_sems.at[0, side],
            recv_sem=halo_sems.at[1, side],
            device_id={"node": (node + by) % groups},
        )

    to_below = halo(low_own, low_box, 0, groups - 1)
    to_above = halo(high_own, high_box, 1, 1)

    def dq_copy(target, source, piece):
        at = pl.ds(pl.multiple_of(piece * tile, tile), tile)
        return pltpu.make_async_remote_copy(
            src_ref=dq_own.at[target, at],
            dst_ref=dq_box.at[source, at],
            send_sem=dq_sems.at[0, target, piece],
            recv_sem=dq_sems.at[1, source, piece],
            device_id={"head": target},
        )

    dkv_spread = Spread(
        along("head"), lambda o: dkv_own.at[o], lambda i: dkv_box.at[i], dkv_sems.at[0], dkv_sems.at[1]
    )

    @pl.when(step == 0)
    def _():
        meet(["head", "node"])
        over_heads.all("start")
        head_box[head] = pair_sum[head]

    @pl.when(step == HEAD_STEP)
    def _():
        over_heads.all("arrived")

        def add(z):
            across_own[z] = sum(head_box[h, z].astype(f32) for h in range(heads)).astype(bf16)

        each(count, add, 0)
        over_pairs.all("start")
        across_box[across[1]] = across_own[across[1]]

    @pl.when(part == 0)
    def _():
        dk[...] = jnp.zeros_like(dk)
        dv[...] = jnp.zeros_like(dv)

    grad = d_ref[...]
    wide = grad.astype(f32)
    inverse = mix_ref[:, HD : HD + 1]
    delta = jnp.sum(wide * mix_ref[:, :HD], 1, keepdims=True)
    gain = inverse * (1.0 / math.sqrt(HD))
    q_turned = q_ref[...].T
    d_turned = (wide * inverse).astype(bf16).T
    here = pl.ds(pl.multiple_of(part * tile, tile), tile)
    dq_here = jnp.where(turn == 0, 0.0, dq[here])
    for at in range(0, nodes, chunk):
        cols = slice(at, at + chunk)
        dp = contract(grad, kv_ref[0, cols, HD:], 1, 1)
        e = e_ref[:, cols]
        ds = (e.astype(f32) * ((dp - delta) * gain)).astype(bf16)
        dq_here += contract(ds, kv_ref[0, cols, :HD], 1, 0)
        dk[:, cols] += contract(q_turned, ds, 1, 0)
        dv[:, cols] += contract(d_turned, e, 1, 0)
    dq[here] = dq_here

    for which, own, copy in ((0, low_own, to_below), (1, high_own, to_above)):

        @pl.when(last & (turn == which))
        def _(own=own, copy=copy):
            own[:HD] = dk[...].astype(bf16)
            own[HD:] = dv[...].astype(bf16)
            copy.start()

    @pl.when(turn == 2)
    def _():
        target, piece = part // per, part % per
        at = pl.ds(pl.multiple_of(piece * tile, tile), tile)
        low = dq_here.astype(bf16)
        dq_own[target, at] = low

        @pl.when(target == head)
        def _():
            dq_box[head, at] = low

        @pl.when(target != head)
        def _():
            dq_copy(target, head, piece).start()

    @pl.when(last & (turn == 2))
    def _():
        to_below.wait()
        to_above.wait()
        for h in range(heads):
            cols = slice(h * rows, (h + 1) * rows)
            for half, acc in enumerate((dk, dv)):
                lines = slice(half * HD, (half + 1) * HD)
                total = acc[:, cols] + low_box[lines, cols].astype(f32) + high_box[lines, cols].astype(f32)
                dkv_own[h, lines] = total.astype(bf16)
        dkv_spread.all("start")
        dkv_box[head] = dkv_own[head]
        over_pairs.all("arrived")
        total = sum(across_box[z].astype(f32) for z in range(count))
        share_ref[...] = total
        share_low[...] = total.astype(bf16)
        over_full.all("start")
        full[place, pair] = total.astype(bf16)
        grad_q = sum(
            contract(norm_ref[h * rows : (h + 1) * rows], dq_own[h], 0, 0) for h in range(heads)
        )
        grad_kv = sum(
            contract(dkv_own[h], norm_ref[h * rows : (h + 1) * rows], 1, 0) for h in range(heads)
        )
        grad_ref[:, :HD] = grad_q
        grad_ref[:, HD:] = grad_kv.T

        def finish(off):
            other = (head + off) % heads
            for p in range(per):
                dq_copy(other, other, p).wait_recv()
                dq_copy(other, head, p).wait_send()

        each(heads, finish)
        over_full.all("arrived")
        swap(place).start()
        dkv_spread.all("arrived")
        dq_ref[...] = dq_box[...]
        dkv_ref[...] = dkv_box[...]
        swap(place).wait_send()
        swap(1 - place).wait_recv()
        for c in range(2):
            for z in range(count):
                full_ref[z, c] = full[c, z]
        for spread in (dkv_spread, over_heads, over_pairs, over_full):
            spread.all("sent")


def attend_back(query, grad, mix, e, keyval, norm_all, pair_sum, heads, tile, chunk):
    nodes, reach = e.shape
    rows, width = nodes // heads, norm_all.shape[1]
    parts = nodes // tile
    _, count, share, across = pair_sum.shape
    row = lambda width: pl.BlockSpec((tile, width), lambda j, i: (i, 0))
    pair = (heads, count, share, across)
    dma = lambda *shape: pltpu.SemaphoreType.DMA(shape)
    order = lambda j: 2 * j % 3
    return pl.pallas_call(
        functools.partial(attend_back_kernel, chunk=chunk),
        grid=(3, parts),
        in_specs=[
            row(HD),
            row(HD),
            row(2 * HD),
            pl.BlockSpec((tile, nodes), lambda j, i: (i, order(j))),
            pl.BlockSpec((1, nodes, 2 * HD), lambda j, i: (order(j), 0, 0)),
            vmem(),
            vmem(),
        ],
        out_specs=[
            whole((heads, rows, HD)),
            whole((heads, 2 * HD, rows)),
            whole((width, 3 * HD)),
            whole((share, across)),
            whole((count, 2, share, across)),
        ],
        out_shape=[
            jax.ShapeDtypeStruct((heads, rows, HD), bf16),
            jax.ShapeDtypeStruct((heads, 2 * HD, rows), bf16),
            jax.ShapeDtypeStruct((width, 3 * HD), f32),
            jax.ShapeDtypeStruct((share, across), f32),
            jax.ShapeDtypeStruct((count, 2, share, across), bf16),
        ],
        scratch_shapes=[
            pltpu.VMEM((HD, nodes), f32),
            pltpu.VMEM((HD, nodes), f32),
            pltpu.VMEM((nodes, HD), f32),
            *[pltpu.VMEM((2 * HD, nodes), bf16)] * 4,
            *[pltpu.VMEM((heads, rows, HD), bf16)] * 2,
            *[pltpu.VMEM((heads, 2 * HD, rows), bf16)] * 2,
            pltpu.VMEM(pair, bf16),
            *[pltpu.VMEM(pair[1:], bf16)] * 2,
            pltpu.VMEM((share, across), bf16),
            pltpu.VMEM((2, *pair[1:]), bf16),
            dma(2, 2),
            dma(2, heads, rows // tile),
            dma(2, heads),
            dma(2),
            dma(2, heads),
            dma(2, count),
            dma(2, count),
        ],
        compiler_params=remote(60, 5),
        name="attend_back",
    )(query, grad, mix, e, keyval, norm_all, pair_sum)


def middle_kernel(
    place_ref, scale_ref, mixed_ref, zero_ref, wa_ref, wf_ref, mod_ref, wdec_ref, weight_ref,
    node_ref, read_ref, target_ref, eps_ref,
    done_ref, dmix_ref, pair_ref, gdec_ref, gmod_ref, loss_ref,
    one_scr, two_scr, norm_scr, up_scr, act_scr, dec_box, hits, turned, total,
    d_own, d_box, dmix_own, dmix_box, grad, big, pair_box,
    dec_sems, d_sems, dmix_sems, pair_sems, out_sems,
    node_tiles, pixel_tiles,
):
    step = pl.program_id(0)
    heads, rows, _ = mixed_ref.shape
    width = zero_ref.shape[1]
    tile = rows // node_tiles
    head = lax.axis_index("head")
    within, _ = pairs()
    place = within[1]
    count, share = pair_ref.shape[1:3]
    pixel_end = node_tiles + pixel_tiles
    others = nearest_first(head, heads)

    def dec_copy(other, slot, t):
        cols = pl.ds(t * tile, tile)
        return pltpu.make_async_remote_copy(
            src_ref=dec_box.at[head, :, cols],
            dst_ref=dec_box.at[slot, :, cols],
            send_sem=dec_sems.at[0, other, t],
            recv_sem=dec_sems.at[1, slot, t],
            device_id={"head": other},
        )

    d_spread = Spread(along("head"), lambda o: d_own.at[o], lambda i: d_box.at[i], d_sems.at[0], d_sems.at[1])

    def dmix_copy(other, slot, t):
        lines = pl.ds(t * tile, tile)
        return pltpu.make_async_remote_copy(
            src_ref=dmix_own.at[other, lines],
            dst_ref=dmix_box.at[slot, lines],
            send_sem=dmix_sems.at[0, other, t],
            recv_sem=dmix_sems.at[1, slot, t],
            device_id={"head": other},
        )

    def pair_copy(h, part):
        cols = (pl.ds(0, 2 * width), pl.ds(2 * width, HD))[part]
        return pltpu.make_async_remote_copy(
            src_ref=big.at[1 - place, h, :, :, cols],
            dst_ref=pair_box.at[h, :, :, cols],
            send_sem=pair_sems.at[0, part, h],
            recv_sem=pair_sems.at[1, part, h],
            device_id=within[2](1 - place),
        )

    def pack(h, cols):
        for c in range(2):
            for z in range(count):
                at = (2 * z + c) * share
                big[c, h, z, :, cols] = grad[h, at : at + share, cols].astype(bf16)

    @pl.when(step == 0)
    def _():
        meet(["head", "node"])
        turned[...] = jnp.zeros_like(turned)
        total[...] = jnp.zeros_like(total)
        loss_ref[...] = jnp.zeros_like(loss_ref)
        gdec_ref[...] = jnp.zeros_like(gdec_ref)
        gmod_ref[...] = jnp.zeros_like(gmod_ref)

    for t in range(node_tiles):

        @pl.when(step == t)
        def _(t=t, lines=slice(t * tile, (t + 1) * tile)):
            h_one = zero_ref[lines] + sum(
                contract(mixed_ref[h, lines], wa_ref[h, :, 3 * HD :], 1, 1) for h in range(heads)
            )
            one_scr[lines] = h_one
            normed, _ = standardize(h_one)
            norm_two = (normed * (1 + mod_ref[2:3]) + mod_ref[3:4]).astype(bf16)
            norm_scr[lines] = norm_two
            h_two = h_one
            for h in range(heads):
                up = contract(norm_two, wf_ref[h, :, :width], 1, 0)
                up_scr[h, lines] = up
                act = (up * jax.nn.sigmoid(up)).astype(bf16)
                act_scr[h, lines] = act
                h_two = h_two + contract(act, wf_ref[h, :, width:], 1, 1)
            two_scr[lines] = h_two
            final = standardize(h_two)[0].astype(bf16)
            high, low = halves(contract(wdec_ref[...], final, 1, 1))
            dec_box[head, :SLIM, lines] = high
            dec_box[head, SLIM:, lines] = low
            for other in others:
                dec_copy(other, head, t).start()

    @pl.when((step >= node_tiles) & (step < pixel_end))
    def _():
        reads = read_ref[...] - place_ref[0]
        pixels = target_ref.shape[1]
        for h in range(heads):
            spot = lax.broadcasted_iota(jnp.int32, (rows, pixels), 0) + h * rows
            hit = sum((spot == reads[k : k + 1]).astype(f32) for k in range(3)).astype(bf16)
            hits[h * rows : (h + 1) * rows] = hit

        @pl.when(step == node_tiles)
        def _():
            for other in others:
                for t in range(node_tiles):
                    dec_copy(other, other, t).wait_recv()

        field = sum(contract(dec_box[h], hits[h * rows : (h + 1) * rows], 1, 0) for h in range(heads))
        field = (field[:VARS] + field[SLIM : SLIM + VARS]) / 3.0
        target = target_ref[...]
        noisy = target + scale_ref[0] * eps_ref[...]
        error = scale_ref[2] * noisy + scale_ref[3] * field - target
        valid = (node_ref[...] - place_ref[0] < place_ref[2]).astype(f32)
        weighted = valid * weight_ref[:, 0:1]
        loss_ref[:VARS] += fold_lanes(weighted * error * error)
        high, low = halves(scale_ref[4] * weighted * error)
        turned[:VARS] = high
        turned[SLOT : SLOT + VARS] = low
        total[...] += contract(hits[...], turned[...], 1, 1)

    @pl.when(step == pixel_end - 1)
    def _():
        for h in range(heads):
            lines = slice(h * rows, (h + 1) * rows)
            d_own[h] = (total[lines, :SLOT] + total[lines, SLOT:]).astype(bf16)
        for other in others:
            d_spread.copy(other, head).start()
        d_box[head] = d_own[head]

    for t in range(node_tiles):
        final_tile = t == node_tiles - 1

        @pl.when(step == pixel_end + t)
        def _(t=t, lines=slice(t * tile, (t + 1) * tile), final_tile=final_tile):
            normed_two, inv_two = standardize(two_scr[lines])
            final = normed_two.astype(bf16)
            normed_one, inv_one = standardize(one_scr[lines])
            if t == 0:
                for other in others:
                    d_spread.copy(other, other).wait_recv()
            d_dec = sum(d_box[h, lines].astype(f32) for h in range(heads)).astype(bf16)[:, :SLIM]
            gdec_ref[...] += contract(d_dec, final, 0, 0)
            d_two = norm_back(normed_two, inv_two, contract(d_dec, wdec_ref[...], 1, 0))
            d_low = d_two.astype(bf16)
            norm_two = norm_scr[lines]
            d_mid = jnp.zeros_like(d_two)

            def add(h, cols, value):
                if t == 0:
                    grad[h, :, cols] = value
                else:
                    grad[h, :, cols] += value

            for h in range(heads):
                up = up_scr[h, lines]
                d_act = contract(d_low, wf_ref[h, :, width:], 1, 0)
                gating = jax.nn.sigmoid(up)
                d_up = (d_act * gating * (1 + up * (1 - gating))).astype(bf16)
                add(h, slice(0, width), contract(norm_two, d_up, 0, 0))
                add(h, slice(width, 2 * width), contract(d_low, act_scr[h, lines], 0, 0))
                if final_tile:
                    pack(h, slice(0, 2 * width))
                    pair_copy(h, 0).start()
                d_mid += contract(d_up, wf_ref[h, :, :width], 1, 1)
            gmod_ref[0:1] += jnp.sum(d_mid * normed_one, 0, keepdims=True)
            gmod_ref[1:2] += jnp.sum(d_mid, 0, keepdims=True)
            d_one = d_two + norm_back(normed_one, inv_one, d_mid * (1 + mod_ref[2:3]))
            done_ref[lines] = d_one
            one_low = d_one.astype(bf16)
            for h in range(heads):
                dmix_own[h, lines] = contract(one_low, wa_ref[h, :, 3 * HD :], 1, 0).astype(bf16)
            for other in others:
                dmix_copy(other, head, t).start()
            dmix_box[head, lines] = dmix_own[head, lines]
            for h in range(heads):
                add(h, slice(2 * width, 2 * width + HD), contract(one_low, mixed_ref[h, lines], 0, 0))
                if final_tile:
                    pack(h, slice(2 * width, 2 * width + HD))
                    pair_copy(h, 1).start()
            if final_tile:
                for h in range(heads):
                    for part in range(2):
                        pair_copy(h, part).wait_recv()
                    for z in range(count):
                        pair_ref[h, z] = (
                            big[place, h, z].astype(f32) + pair_box[h, z].astype(f32)
                        ).astype(bf16)
                for other in others:
                    for u in range(node_tiles):
                        dmix_copy(other, other, u).wait_recv()
                dmix_ref[...] = dmix_box[...]
                for other in others:
                    d_spread.copy(other, head).wait_send()
                    for u in range(node_tiles):
                        dec_copy(other, head, u).wait_send()
                        dmix_copy(other, head, u).wait_send()
                for h in range(heads):
                    for part in range(2):
                        pair_copy(h, part).wait_send()


def middle(place, scales, mixed, h_zero, w_attn, w_ffn, modulation, w_dec, weight, node_row, read_rows, target, eps, groups):
    heads, rows, _ = mixed.shape
    width = h_zero.shape[1]
    node_tiles, pixels = 2, target.shape[1] // heads
    tile = 512
    pixel_tiles = pixels // tile
    share, count = width // groups, groups // 2
    grads = 2 * width + HD
    pair = (heads, count, share, grads)
    low = lambda *shape: pltpu.VMEM(shape, bf16)
    full = lambda *shape: pltpu.VMEM(shape, f32)
    dma = lambda *shape: pltpu.SemaphoreType.DMA(shape)

    def at(i):
        part = jnp.clip(i - node_tiles, 0, pixel_tiles - 1)
        return 0, lax.axis_index("head") * pixel_tiles + part

    piece = lambda lines: pl.BlockSpec((lines, tile), at)
    return pl.pallas_call(
        functools.partial(middle_kernel, node_tiles=node_tiles, pixel_tiles=pixel_tiles),
        grid=(2 * node_tiles + pixel_tiles,),
        in_specs=[smem(), smem()] + [vmem()] * 7 + [piece(1), piece(3), piece(VARS), piece(VARS)],
        out_specs=[
            whole((rows, width)),
            whole((heads, rows, HD)),
            whole(pair),
            whole((SLIM, width)),
            whole((8, width)),
            whole((SLIM, 128)),
        ],
        out_shape=[
            jax.ShapeDtypeStruct((rows, width), f32),
            jax.ShapeDtypeStruct((heads, rows, HD), bf16),
            jax.ShapeDtypeStruct(pair, bf16),
            jax.ShapeDtypeStruct((SLIM, width), f32),
            jax.ShapeDtypeStruct((8, width), f32),
            jax.ShapeDtypeStruct((SLIM, 128), f32),
        ],
        scratch_shapes=[
            full(rows, width),
            full(rows, width),
            low(rows, width),
            full(heads, rows, width),
            low(heads, rows, width),
            low(heads, 2 * SLIM, rows),
            low(heads * rows, tile),
            low(2 * SLOT, tile),
            full(heads * rows, 2 * SLOT),
            low(heads, rows, SLOT),
            low(heads, rows, SLOT),
            low(heads, rows, HD),
            low(heads, rows, HD),
            full(heads, width, grads),
            low(2, *pair),
            low(*pair),
            dma(2, heads, node_tiles),
            dma(2, heads),
            dma(2, heads, node_tiles),
            dma(2, 2, heads),
            dma(2, heads),
        ],
        compiler_params=remote(62, 7),
        name="middle",
    )(
        place, scales, mixed, h_zero, w_attn, w_ffn, modulation, w_dec, weight, node_row, read_rows, target, eps
    )


def settle_kernel(
    feat_ref, dq_ref, dkv_ref, w_ref, zero_ref, done_ref, in_ref, mod_ref, gdec_ref, gmod_ref, qkv_ref, big_ref, loss_ref,
    small_ref, share_ref, full_ref, sums_ref,
    q_low, q_pair, q_sum, q_box, q_share, q_full,
    parts, part_box, part_sum, part_own, pay, heard, tally, tallies,
    pair_sems, q_sems, f_sems, a_sems, n_sems, b_sems, t_sems,
):
    heads, width = w_ref.shape[0], w_ref.shape[1]
    share_rows = share_ref.shape[0]
    head, node = lax.axis_index("head"), lax.axis_index("node")
    groups = heard.shape[0]
    within, across = pairs()
    place, pair, count = within[1], across[1], across[0]

    def to_other(source, target, index):
        return pltpu.make_async_remote_copy(
            src_ref=source,
            dst_ref=target,
            send_sem=pair_sems.at[0, index],
            recv_sem=pair_sems.at[1, index],
            device_id=within[2](1 - place),
        )

    for c in range(2):
        for z in range(count):
            at = (2 * z + c) * share_rows
            q_low[c, z] = qkv_ref[at : at + share_rows].astype(bf16)
    meet(["head", "node"])
    q_pairs = to_other(q_low.at[1 - place], q_pair, 0)
    q_pairs.start()

    d_norm = sum(
        contract(dq_ref[h], w_ref[h, :, :HD], 1, 1)
        + contract(dkv_ref[h], w_ref[h, :, HD : 3 * HD], 0, 1)
        for h in range(heads)
    )
    normed, inv = standardize(zero_ref[...])
    d_zero = done_ref[...] + norm_back(normed, inv, d_norm * (1 + mod_ref[0:1]))

    q_pairs.wait()
    for z in range(count):
        q_sum[z] = (q_low[place, z].astype(f32) + q_pair[z].astype(f32)).astype(bf16)
    q_over = Spread(across, lambda o: q_sum.at[o], lambda i: q_box.at[i], q_sems.at[0], q_sems.at[1])
    q_over.all("start")
    q_box[pair] = q_sum[pair]

    g_enc = contract(in_ref[...].T, d_zero, 1, 0, highest)
    parts[...] = jnp.zeros_like(parts)
    flat = parts.reshape(parts.shape[0] * parts.shape[1], width)
    flat[:VARS] = g_enc[:VARS]
    flat[VARS : 2 * VARS] = g_enc[SLOT : SLOT + VARS]
    flat[2 * VARS : 3 * VARS] = gdec_ref[:VARS]
    at = 3 * VARS
    flat[at : at + 1] = jnp.sum(d_norm * normed, 0, keepdims=True)
    flat[at + 1 : at + 2] = jnp.sum(d_norm, 0, keepdims=True)
    flat[at + 2 : at + 4] = gmod_ref[0:2]
    over_heads = Spread(
        along("head"), lambda o: parts.at[o], lambda i: part_box.at[i], a_sems.at[0], a_sems.at[1]
    )
    over_heads.all("start")
    part_box[head] = parts[head]

    q_over.all("arrived")
    share = sum(q_box[z].astype(f32) for z in range(count))
    share_ref[...] = share
    q_share[...] = share.astype(bf16)
    q_full[place, pair] = share.astype(bf16)
    f_over = Spread(
        across, lambda _: q_share, lambda i: q_full.at[place, i], f_sems.at[0], f_sems.at[1]
    )
    f_over.all("start")

    over_heads.all("arrived")
    total = sum(part_box[h] for h in range(heads))
    for t in range(groups):
        part_sum[t] = total[8 * t : 8 * t + 8]
    over_nodes = Spread(
        along("node"), lambda o: part_sum.at[o], lambda i: part_own.at[i], n_sems.at[0], n_sems.at[1]
    )
    over_nodes.all("start")
    part_own[node] = part_sum[node]

    squares = jnp.sum(share * share) + jnp.sum(big_ref[...] * big_ref[...])
    loss = jnp.sum(loss_ref[:VARS])
    over_nodes.all("arrived")
    own = sum(part_own[t] for t in range(groups))
    row = lax.broadcasted_iota(jnp.int32, own.shape, 0) + 8 * (head * groups + node)
    squares += jnp.sum(own * own * jnp.where(row >= 3 * VARS, feat_ref[0], 1.0))
    line = lax.broadcasted_iota(jnp.int32, (8, 128), 0)
    pay[:, :width] = own
    pay[:, width:] = jnp.where(line == 0, squares, jnp.where(line == 1, loss, 0.0))
    back = Spread(along("node"), lambda _: pay, lambda i: heard.at[i], b_sems.at[0], b_sems.at[1])
    back.all("start")
    heard[node] = pay[...]

    f_over.all("arrived")
    q_rest = to_other(q_full.at[place], q_full.at[place], 1)
    q_rest.start()

    back.all("arrived")
    tally[...] = sum(heard[t, :, width:] for t in range(groups))
    tell = Spread(along("head"), lambda _: tally, lambda i: tallies.at[i], t_sems.at[0], t_sems.at[1])
    tell.all("start")
    tallies[head] = tally[...]
    for t in range(groups):
        small_ref[8 * t : 8 * t + 8] = heard[t, :, :width]
    tell.all("arrived")
    sums_ref[...] = sum(tallies[h] for h in range(heads))

    q_rest.wait_send()
    to_other(q_full.at[1 - place], q_full.at[1 - place], 1).wait_recv()
    for c in range(2):
        for z in range(count):
            full_ref[2 * z + c] = q_full[c, z]
    for spread in (q_over, over_heads, f_over, over_nodes, back, tell):
        spread.all("sent")


def settle(feat_sq, dq, dkv, w_attn, h_zero, d_one, node_in, modulation, grad_dec, gmod_two, grad_qkv, big_share, loss, groups):
    heads, rows, _ = dq.shape
    width = h_zero.shape[1]
    count = groups // 2
    share = (grad_qkv.shape[0] // groups, grad_qkv.shape[1])
    low = lambda *shape: pltpu.VMEM(shape, bf16)
    full = lambda *shape: pltpu.VMEM(shape, f32)
    dma = lambda *shape: pltpu.SemaphoreType.DMA(shape)
    return pl.pallas_call(
        settle_kernel,
        in_specs=[smem()] + [vmem()] * 12,
        out_specs=[vmem()] * 4,
        out_shape=[
            jax.ShapeDtypeStruct((8 * groups, width), f32),
            jax.ShapeDtypeStruct(share, f32),
            jax.ShapeDtypeStruct((groups, *share), bf16),
            jax.ShapeDtypeStruct((8, 128), f32),
        ],
        scratch_shapes=[
            low(2, count, *share),
            low(count, *share),
            low(count, *share),
            low(count, *share),
            low(*share),
            low(2, count, *share),
            full(heads, 8 * groups, width),
            full(heads, 8 * groups, width),
            full(groups, 8, width),
            full(groups, 8, width),
            full(8, width + 128),
            full(groups, 8, width + 128),
            full(8, 128),
            full(heads, 8, 128),
            dma(2, 2),
            dma(2, count),
            dma(2, count),
            dma(2, heads),
            dma(2, groups),
            dma(2, groups),
            dma(2, heads),
        ],
        compiler_params=remote(56, 1),
        name="settle",
    )(feat_sq, dq, dkv, w_attn, h_zero, d_one, node_in, modulation, grad_dec, gmod_two, grad_qkv, big_share, loss)


def eliminate(work, done):
    count = work.shape[0]
    lane = lax.broadcasted_iota(jnp.int32, (1, BLOCK), 1)
    sub = lax.broadcasted_iota(jnp.int32, (STRIP, BLOCK), 0)
    pivots = [jnp.ones((1, BLOCK), f32) for _ in range(count)]
    both = lambda x: jnp.concatenate([x, x], 1)
    for at in range(0, BLOCK, STRIP):
        strip = slice(at, at + STRIP)
        rows = [work[m, strip] for m in range(count)]
        columns = [
            [jnp.broadcast_to(rows[m][:, at + k : at + k + 1], (STRIP, BLOCK)) for k in range(STRIP)]
            for m in range(count)
        ]
        scale = [jnp.ones((STRIP, BLOCK), f32) for _ in range(count)]
        for r in range(STRIP):
            for m in range(count):
                column = columns[m][r]
                pivot = jnp.broadcast_to(column[r : r + 1], (STRIP, BLOCK))
                factor = jnp.where(sub > r, column * (1.0 / pivot), 0.0)
                scale[m] = jnp.where(sub == r, pivot, scale[m])
                for k in range(r + 1, STRIP):
                    columns[m][k] = columns[m][k] - factor * columns[m][k][r : r + 1]
                pivots[m] = jnp.where(lane == at + r, pivot[:1], pivots[m])
                rows[m] = rows[m] - both(factor) * rows[m][r : r + 1]
        for m in range(count):
            done[m, strip] = rows[m][:, BLOCK:]
            if at + STRIP < BLOCK:
                high, mid, low = thirds(rows[m] * both(lax.rsqrt(scale[m])))
                left = jnp.concatenate([high, high, mid, mid, high, low], 0)[:, :BLOCK]
                right = jnp.concatenate([high, mid, high, mid, low, high], 0)
                rest = slice(at + STRIP, BLOCK)
                work[m, rest] -= contract(left, right, 0, 0)[rest]
    return pivots


def renew_kernel(gram_ref, product_ref, small_ref, out_ref, all_ref, gram, both, work, done, box, sems):
    count, size = gram_ref.shape[:2]
    k = pl.program_id(0)

    head = lax.axis_index("head")
    smalls = Spread(along("head"), lambda _: small_ref, lambda i: box.at[i], sems.at[0], sems.at[1])

    @pl.when(k == 0)
    def _():
        gram[...] = gram_ref[...]
        both[...] = product_ref[...]
        meet(["head"])
        smalls.all("start")
        box[head] = small_ref[...]

    @pl.when(k == pl.num_programs(0) - 1)
    def _():
        smalls.all("arrived")
        all_ref[...] = box[...]
        smalls.all("sent")

    at = pl.ds(pl.multiple_of(k * BLOCK, BLOCK), BLOCK)
    unit = lax.broadcasted_iota(jnp.int32, (BLOCK, BLOCK), 0) == lax.broadcasted_iota(
        jnp.int32, (BLOCK, BLOCK), 1
    )
    for m in range(count):
        work[m, :, :BLOCK] = gram[m, at, at]
        work[m, :, BLOCK:] = unit.astype(f32)
    roots = [lax.rsqrt(p) for p in eliminate(work, done)]
    for step in range(size // BLOCK):

        @pl.when(k == step)
        def _(here=slice(step * BLOCK, (step + 1) * BLOCK), rest=(step + 1) * BLOCK):
            for m in range(count):
                factor = done[m]
                panel = contract(both[m, :, here], factor, 1, 1, highest) * roots[m]
                out_ref[m] = panel
                if rest < size:
                    left = contract(gram[m, rest:, here], factor, 1, 1, highest) * roots[m]
                    both[m, :, rest:] -= contract(panel, left, 1, 1, highest)
                    gram[m, rest:, rest:] -= contract(left, left, 1, 1, highest)


def renew(gram, product, small, heads):
    count, size = gram.shape[:2]
    gathered = (heads, *small.shape)
    return pl.pallas_call(
        renew_kernel,
        grid=(size // BLOCK,),
        in_specs=[whole(gram.shape), whole(gram.shape), whole(small.shape)],
        out_specs=[pl.BlockSpec((count, size, BLOCK), lambda k: (0, 0, k)), whole(gathered)],
        out_shape=[jax.ShapeDtypeStruct(gram.shape, f32), jax.ShapeDtypeStruct(gathered, f32)],
        scratch_shapes=[
            pltpu.VMEM((count, size, size), f32),
            pltpu.VMEM((count, size, size), f32),
            pltpu.VMEM((count, BLOCK, 2 * BLOCK), f32),
            pltpu.VMEM((count, BLOCK, BLOCK), f32),
            pltpu.VMEM(gathered, f32),
            pltpu.SemaphoreType.DMA((2, heads)),
        ],
        compiler_params=remote(48, 6),
        name="renew",
    )(gram, product, small)


def local(
    prev_state,
    target,
    noise_eps,
    noise_level,
    valid_count,
    neighbours,
    nbr_count,
    pix_node,
    pix_read,
    w_enc,
    w_cond,
    w_dec,
    layer_w,
    soap_first,
    soap_second,
    soap_basis,
    soap_stats,
    enc_first,
    enc_second,
    cond_first,
    cond_second,
    dec_first,
    dec_second,
):
    nodes = nbr_count.shape[0]
    groups = lax.axis_size("node")
    heads = lax.axis_size("head")
    rows = nodes // heads
    block_start = lax.axis_index("node") * nodes
    quarter = lax.axis_index("head")
    width = w_enc.shape[1]
    both = ("head", "node")

    low_w = layer_w.astype(bf16)
    ffn_share = jnp.concatenate([low_w[1], low_w[2]], 1)
    noise_sigma, noise_feat = noise_terms(noise_level)
    sig_sq = noise_sigma * noise_sigma
    input_scale = lax.rsqrt(sig_sq + 1.0)
    skip_scale = 1.0 / (sig_sq + 1.0)
    output_scale = noise_sigma * lax.rsqrt(sig_sq + 1.0)
    loss_scale = (sig_sq + 1.0) / sig_sq
    modulation = jnp.dot(noise_feat[None, :], w_cond, precision=highest).reshape(4, width)

    prev_t, target_t, eps_t = prev_state.T, target.T, noise_eps.T
    node_row = pix_node.reshape(1, -1)
    read_rows = pix_read.T
    place = jnp.stack([block_start, quarter * rows, valid_count[0], quarter]).astype(jnp.int32)
    node_in, stat, column, w_attn = encode(
        place, jnp.stack([noise_sigma, input_scale]), node_row, prev_t, target_t, eps_t, low_w[0], rows, 1024, groups
    )
    w_attn = w_attn.reshape(width, -1)

    pad_enc = jnp.zeros((2, SLOT, width), bf16)
    pad_enc = pad_enc.at[:, :VARS].set(w_enc.astype(bf16).reshape(2, VARS, width))
    h_zero, norm_all, query, keyval, stat, counts = open_nodes(
        node_in, pad_enc.reshape(2 * SLOT, width), modulation, stat, w_attn, neighbours.T,
        nbr_count.reshape(1, -1), heads, groups,
    )
    norm_all, query = norm_all.reshape(nodes, -1), query.reshape(nodes, -1)
    keyval = keyval.reshape(3, nodes, -1)
    stat_sum = stat[:, 0]
    count_sum = stat_sum[SLIM - 1]
    var_weight = 1.0 / (stat_sum[:VARS] / count_sum + norm_eps)
    loss_count = count_sum * VARS
    e, mix, mixed, attn_all, ffn_all = attend(query, keyval, counts, column, ffn_share, heads, 128, 512)
    attn_all = attn_all.reshape(heads, width, -1)
    ffn_all = ffn_all.reshape(heads, width, -1)

    w_dec_t = jnp.zeros((SLIM, width), bf16).at[:VARS].set(w_dec.T.astype(bf16))
    scales = jnp.stack(
        [noise_sigma, input_scale, skip_scale, output_scale, output_scale * (2.0 / loss_count) / 3.0]
    )
    weight = jnp.broadcast_to((loss_scale * var_weight)[:, None], (VARS, 128))
    d_one, d_mixed, pair_sum, grad_dec, gmod_two, loss_part = middle(
        place, scales, mixed, h_zero, attn_all, ffn_all, modulation, w_dec_t, weight, node_row, read_rows,
        target_t, eps_t, groups,
    )
    d_mixed = d_mixed.reshape(nodes, HD)
    dq, dkv, grad_qkv, big_share, big_full = attend_back(
        query, d_mixed, mix, e, keyval, norm_all, pair_sum, heads, 256, 512
    )
    feat_sq = jnp.sum(noise_feat * noise_feat).reshape(1)
    small, qkv_share, qkv_full, sums = settle(
        feat_sq, dq, dkv, attn_all, h_zero, d_one, node_in, modulation, grad_dec, gmod_two, grad_qkv, big_share,
        loss_part, groups,
    )
    big_full = big_full.reshape(width, -1)
    layer_share = jnp.stack(
        [
            jnp.concatenate([qkv_share, big_share[:, 2 * width :]], 1),
            big_share[:, :width],
            big_share[:, width : 2 * width],
        ]
    )
    grad_norm = jnp.sqrt(sums[0, 0])
    loss_sum = sums[1, 0]
    clip_factor = clip_limit / jnp.maximum(grad_norm, clip_limit)
    clipped = clip_factor * layer_share
    grad_full = jnp.stack(
        [
            jnp.concatenate([qkv_full.reshape(width, -1), big_full[:, 2 * width :]], 1),
            big_full[:, :width],
            big_full[:, width : 2 * width],
        ]
    )
    raw_stat = jnp.einsum("idb,idc->ibc", grad_full, grad_full, preferred_element_type=f32)
    stat_new = clip_factor * (clip_factor * raw_stat)
    basis_old = soap_basis[:, 0]
    rotated = jnp.einsum("idb,ibc->idc", clipped, basis_old, precision=highest)
    first_new = beta_first * soap_first + (1 - beta_first) * rotated
    second_new = beta_second * soap_second + (1 - beta_second) * rotated * rotated
    direction = (
        first_new
        / (1 - beta_first**STEP)
        / (jnp.sqrt(second_new / (1 - beta_second**STEP)) + adam_epsilon)
    )
    step_back = jnp.einsum("idc,ibc->idb", direction, basis_old, precision=highest)
    layer_new = layer_w - rate_layer * (step_back + decay_rate * layer_w)
    stats_new = beta_stats * soap_stats[:, 0] + (1 - beta_stats) * stat_new
    product = jnp.einsum("ibc,icd->ibd", stats_new, basis_old, precision=highest)
    gram_matrix = jnp.einsum("ibc,ibd->icd", product, product, precision=highest)
    basis_new, small = renew(gram_matrix, product, small, heads)
    small = small.reshape(-1, width)
    grad_enc = small[: 2 * VARS]
    grad_dec = small[2 * VARS : 3 * VARS]
    grad_cond = noise_feat[:, None] * small[3 * VARS : 3 * VARS + 4].reshape(1, -1)
    enc_new = adam_small(w_enc, clip_factor * grad_enc, enc_first, enc_second)
    cond_new = adam_small(w_cond, clip_factor * grad_cond, cond_first, cond_second)
    dec_new = adam_small(w_dec.T, clip_factor * grad_dec, dec_first.T, dec_second.T)
    return (
        jnp.reshape(loss_sum, (1,)),
        jnp.reshape(loss_count, (1,)),
        jnp.reshape(grad_norm, (1,)),
        layer_new,
        first_new,
        second_new,
        basis_new[:, None],
        stats_new[:, None],
        *enc_new,
        *cond_new,
        *(x.T for x in dec_new),
    )


def solution(mesh):
    pixel = P("node", None)
    layer = P(None, "node", "head")
    basis = P(None, "head", None, None)
    placed = (
        *(pixel,) * 3,
        P(),
        P("node"),
        P("node", None),
        P("node"),
        P("node"),
        P("node", None),
        *(P(),) * 3,
        *(layer,) * 3,
        *(basis,) * 2,
        *(P(),) * 6,
    )
    return jax.shard_map(
        local,
        mesh=mesh,
        in_specs=placed,
        out_specs=(*(P(),) * 3, *(layer,) * 3, *(basis,) * 2, *(P(),) * 9),
        check_vma=False,
    )
```

profile of v0, /device:TPU:0, one launch (start us, length us, event | category | flops | bytes accessed | tf_op | source)
XLA Modules:
  0.0 380.6 jit_solution(15376864953740691125)
XLA Ops:
  2.2 1.0 convert_element_type.18
  3.3 2.2 copy-done
  5.5 0.8 copy-done.4
  6.3 16.3 %encode.1 = (f32[512,256]{1,0:T(8,128)S(1)}, f32[96,128]{1,0:T(8,128)S(1)}, bf16[4,64,512]{2,1,0:T(8,128)(2,1)S(1)}, bf16[4,2,64,512]{3,2,1,0:T(8,128)(2,1)S(1)}) custom-call(s32[4]{0:T(128)S(1)} %pad_add_fusion.place_ref, f32[2]{0:T(128)S(1)} %pad_maximum_fusion.2.scale_ref, s32[1,12288]{1,0:T(1,128)S(1)} %bitcast.132, f32[84,12288]{1,0:T(8,128)S(1)} %bitcast.125, ...), custom_call_target="tpu_custom_call" | custom-call | tf_op jit(solution)/shard_map/encode/pallas_call | solution.py:260
  22.6 0.8 copy-done.1
  23.4 0.8 copy-done.2
  27.9 41.3 %open_nodes.1 = (f32[512,512]{1,0:T(8,128)}, bf16[4,512,512]{2,1,0:T(8,128)(2,1)}, bf16[4,512,128]{2,1,0:T(8,128)(2,1)}, bf16[3,4,512,256]{3,2,1,0:T(8,128)(2,1)...) custom-call(f32[512,256]{1,0:T(8,128)} %copy-done.1, bf16[256,512]{1,0:T(8,128)(2,1)} %bitcast.149, f32[4,512]{1,0:T(4,128)} %bitcast.153, ...), custom_call_target="tpu_custom_call" | custom-call | tf_op jit(solution)/shard_map/open_nodes/pallas_call | solution.py:418
  69.9 54.2 %attend.1 = (bf16[2048,6144]{1,0:T(8,128)(2,1)}, f32[2048,256]{1,0:T(8,128)}, bf16[4,512,128]{2,1,0:T(8,128)(2,1)}, bf16[4,4,2,64,512]{4,3,2,1,0:T(8,128)(2,1)}, bf16[4,4,2,64,1024]{4,3,2,1,0:T(8,128)(2,1)}) custom-call(bf16[2048,128]{1,0:T(8,128)(2,1)} %bitcast.143, bf16[3,2048,256]{2,1,0:T(8,128)(2,1)} %bitcast.137, ...), custom_call_target="tpu_custom_call" | custom-call | tf_op jit(solution)/shard_map/attend/pallas_call | solution.py:590
  124.7 0.8 multiply_reduce_fusion
  128.2 73.4 %middle.1 = (f32[512,512]{1,0:T(8,128)}, bf16[4,512,128]{2,1,0:T(8,128)(2,1)}, bf16[4,4,64,1152]{3,2,1,0:T(8,128)(2,1)}, f32[96,512]{1,0:T(8,128)}, f32[8,512]{1,0:T(8,128)}, /*index=5*/f32[96,128]{1,0:T(8,128)}) custom-call(s32[4]{0:T(128)} %copy-done.7, f32[5]{0:T(128)} %stack.66.scale_ref, bf16[4,512,128]{2,1,0:T(8,128)(2,1)} %get-tuple-element.81.mixed_ref, ...), custom_call_target="tpu_custom_call" | custom-call | tf_op jit(solution)/shard_map/middle/pallas_call | solution.py:1075
  201.6 73.6 %attend_back.1 = (bf16[4,512,128]{2,1,0:T(8,128)(2,1)}, bf16[4,256,512]{2,1,0:T(8,128)(2,1)}, f32[512,384]{1,0:T(8,128)}, f32[64,1152]{1,0:T(8,128)}, bf16[4,2,64,1152]{3,2,1,0:T(8,128)(2,1)}) custom-call(bf16[2048,128]{1,0:T(8,128)(2,1)} %bitcast.144, bf16[2048,128]{1,0:T(8,128)(2,1)} %bitcast.150, f32[2048,256]{1,0:T(8,128)} %get-tuple-element.86.mix_ref, ...), custom_call_target="tpu_custom_call" | custom-call | tf_op jit(solution)/shard_map/attend_back/pallas_call | solution.py:805
  275.2 34.5 %settle.1 = (f32[64,512]{1,0:T(8,128)}, f32[64,384]{1,0:T(8,128)}, bf16[8,64,384]{2,1,0:T(8,128)(2,1)}, f32[8,128]{1,0:T(8,128)}) custom-call(f32[1]{0:T(128)} %bitcast.1.feat_ref, bf16[4,512,128]{2,1,0:T(8,128)(2,1)} %get-tuple-element.90.dq_ref, bf16[4,256,512]{2,1,0:T(8,128)(2,1)} %get-tuple-element.91.dkv_ref, bf16[4,512,512]{2,1,0:T(8,128)(2,1)} %bitcast.140, ...), custom_call_target="tpu_custom_call" | custom-call | tf_op jit(solution)/shard_map/settle/pallas_call | solution.py:1251
  309.7 1.2 maximum_bitcast_fusion
  311.0 1.3 fusion.55
  313.0 1.3 bitcast_add_fusion
  314.9 5.3 %fusion.product_ref = f32[3,512,512]{2,1,0:T(8,128)S(1)} fusion(f32[3,512,512]{2,1,0:T(8,128)S(1)} %bitcast_add_fusion, f32[3,1,512,512]{3,2,1,0:T(8,128)S(1)} %copy-done.9), kind=kOutput, calls=%fused_computation.2 | convolution fusion | flops 4831838208 | bytes 9437184 | tf_op jit(solution)/shard_map/ibc,icd->ibd/dot_general | solution.py:1509
  320.2 6.9 %fusion.56.gram_ref = f32[3,512,512]{2,1,0:T(8,128)} fusion(f32[3,512,512]{2,1,0:T(8,128)S(1)} %fusion.product_ref), kind=kOutput, calls=%fused_computation.85 | convolution fusion | flops 4831838208 | bytes 6291456 | tf_op jit(solution)/shard_map/ibc,ibd->icd/dot_general | solution.py:1510
  327.2 40.0 %renew.1 = (f32[3,512,512]{2,1,0:T(8,128)S(1)}, f32[4,64,512]{2,1,0:T(8,128)S(1)}) custom-call(f32[3,512,512]{2,1,0:T(8,128)} %fusion.56.gram_ref, f32[3,512,512]{2,1,0:T(8,128)} %copy-done.8, f32[64,512]{1,0:T(8,128)S(1)} %copy-done.5), custom_call_target="tpu_custom_call" | custom-call | tf_op jit(solution)/shard_map/renew/pallas_call | solution.py:1370
  367.2 0.9 fusion.44
  368.2 1.1 multiply_subtract_fusion.1
  369.3 1.1 multiply_subtract_fusion
  370.5 2.1 multiply_add_fusion
  372.6 3.9 %fusion.17 = f32[3,64,512]{2,1,0:T(8,128)} fusion(f32[3,64,512]{2,1,0:T(8,128)S(1)} %copy-done.11, f32[3,1,512,512]{3,2,1,0:T(8,128)S(1)} %copy-done.9, f32[3,64,512]{2,1,0:T(8,128)S(1)} %get-tuple-element.202, f32[3,64,512]{2,1,0:T(8,128)S(1)} %get-tuple-element.201), kind=kOutput, calls=%fused_computation.15 | convolution fusion | flops 604766208 | bytes 4718592 | tf_op jit(solution)/shard_map/idc,ibc->idb/dot_general | solution.py:1506
  376.5 1.7 copy.71
  (79 shorter events, 7.8 us)
Async XLA Ops:
  2.2 20.4 %copy-start.7 = (s32[4]{0:T(128)}, s32[4]{0:T(128)S(1)}, u32[]{:S(2)}) copy-start(s32[4]{0:T(128)S(1)} %pad_add_fusion.place_ref) | copy-start | bytes 52
  3.2 2.2 copy-start
  6.3 20.0 %copy-start.17 = (f32[32,2048]{1,0:T(8,128)S(1)}, f32[32,2048]{1,0:T(8,128)}, u32[]{:S(2)}) copy-start(f32[32,2048]{1,0:T(8,128)} %param.37) | copy-start | bytes 786436
  6.3 20.8 %copy-start.14 = (f32[168,512]{1,0:T(8,128)S(1)}, f32[168,512]{1,0:T(8,128)}, u32[]{:S(2)}) copy-start(f32[168,512]{1,0:T(8,128)} %param.36) | copy-start | bytes 1032196
  69.9 54.3 %copy-start.28 = (f32[96,128]{1,0:T(8,128)S(1)}, f32[96,128]{1,0:T(8,128)}, u32[]{:S(2)}) copy-start(f32[96,128]{1,0:T(8,128)} %get-tuple-element.77) | copy-start | bytes 147460
  69.9 57.6 %copy-start.18 = (f32[512,84]{0,1:T(8,128)S(1)}, f32[512,84]{0,1:T(8,128)}, u32[]{:S(2)}) copy-start(f32[512,84]{0,1:T(8,128)} %param.38) | copy-start | bytes 516100
  275.2 34.5 %copy-start.16 = (bf16[4,2,64,1152]{3,2,1,0:T(8,128)(2,1)S(1)}, bf16[4,2,64,1152]{3,2,1,0:T(8,128)(2,1)}, u32[]{:S(2)}) copy-start(bf16[4,2,64,1152]{3,2,1,0:T(8,128)(2,1)} %get-tuple-element.101) | copy-start | bytes 3538948
  309.7 3.3 copy-start.29
  314.9 5.3 %copy-start.10 = (f32[3,512,512]{2,1,0:T(8,128)}, f32[3,512,512]{2,1,0:T(8,128)S(1)}, u32[]{:S(2)}) copy-start(f32[3,512,512]{2,1,0:T(8,128)S(1)} %bitcast_add_fusion) | copy-start | bytes 9437188
  320.2 6.9 %copy-start.8 = (f32[3,512,512]{2,1,0:T(8,128)}, f32[3,512,512]{2,1,0:T(8,128)S(1)}, u32[]{:S(2)}) copy-start(f32[3,512,512]{2,1,0:T(8,128)S(1)} %fusion.product_ref) | copy-start | bytes 9437188
  320.2 6.9 %copy-start.5 = (f32[64,512]{1,0:T(8,128)S(1)}, f32[64,512]{1,0:T(8,128)}, u32[]{:S(2)}) copy-start(f32[64,512]{1,0:T(8,128)} %get-tuple-element.102.small_ref) | copy-start | bytes 393220
  327.1 40.1 %copy-start.25 = (f32[512,84]{0,1:T(8,128)S(1)}, f32[512,84]{0,1:T(8,128)}, u32[]{:S(2)}) copy-start(f32[512,84]{0,1:T(8,128)} %param.49) | copy-start | bytes 516100
  327.1 40.1 %copy-start.26 = (f32[512,84]{0,1:T(8,128)S(1)}, f32[512,84]{0,1:T(8,128)}, u32[]{:S(2)}) copy-start(f32[512,84]{0,1:T(8,128)} %param.48) | copy-start | bytes 516100
  327.1 41.1 %copy-start.23 = (f32[32,2048]{1,0:T(8,128)S(1)}, f32[32,2048]{1,0:T(8,128)}, u32[]{:S(2)}) copy-start(f32[32,2048]{1,0:T(8,128)} %param.46) | copy-start | bytes 786436
  327.1 41.0 %copy-start.24 = (f32[32,2048]{1,0:T(8,128)S(1)}, f32[32,2048]{1,0:T(8,128)}, u32[]{:S(2)}) copy-start(f32[32,2048]{1,0:T(8,128)} %param.47) | copy-start | bytes 786436
  327.1 42.1 %copy-start.21 = (f32[168,512]{1,0:T(8,128)S(1)}, f32[168,512]{1,0:T(8,128)}, u32[]{:S(2)}) copy-start(f32[168,512]{1,0:T(8,128)} %param.44) | copy-start | bytes 1032196
  327.1 42.1 %copy-start.22 = (f32[168,512]{1,0:T(8,128)S(1)}, f32[168,512]{1,0:T(8,128)}, u32[]{:S(2)}) copy-start(f32[168,512]{1,0:T(8,128)} %param.45) | copy-start | bytes 1032196
  367.1 3.3 copy-start.15
  367.2 3.3 copy-start.27
  367.2 3.3 copy-start.19
  367.2 3.3 copy-start.20
  370.4 2.2 copy-start.11
  372.6 5.6 %copy-start.12 = (f32[3,64,512]{2,1,0:T(8,128)}, f32[3,64,512]{2,1,0:T(8,128)S(1)}, u32[]{:S(2)}) copy-start(f32[3,64,512]{2,1,0:T(8,128)S(1)} %get-tuple-element.201) | copy-start | bytes 1179652
  372.6 5.6 %copy-start.13 = (f32[3,64,512]{2,1,0:T(8,128)}, f32[3,64,512]{2,1,0:T(8,128)S(1)}, u32[]{:S(2)}) copy-start(f32[3,64,512]{2,1,0:T(8,128)S(1)} %get-tuple-element.202) | copy-start | bytes 1179652
  (6 other events, 5.6 us)
where the time goes:
time: 387 us; the launch traced here: 381 us
  Pallas kernels  333 us (86%)
  matrix products  19.6 us (5%)
  local copies, waits for them, and re-layouts  13.5 us (3%)
  other arithmetic  7.73 us (2%)
  between operations  6.48 us (2%)
    pallas_call x1, Pallas kernels, attend_back(): pl.pallas_call(functools.partial(attend_back_kernel, chunk=chunk), grid=(...  73.6 us
    pallas_call x1, Pallas kernels, middle(): pl.pallas_call(functools.partial(middle_kernel, node_tiles=node_tiles, pi...  73.4 us
    pallas_call x1, Pallas kernels, attend(): pl.pallas_call(functools.partial(attend_kernel, chunk=chunk), grid=(nodes...  54.2 us
    pallas_call x1, Pallas kernels, open_nodes(): pl.pallas_call(open_kernel, in_specs=[vmem()] * 7, out_specs=[vmem()] * 5...  41.3 us
    pallas_call x1, Pallas kernels, renew(): pl.pallas_call(renew_kernel, grid=(size // BLOCK,), in_specs=[whole(gram....  40 us
    pallas_call x1, Pallas kernels, settle(): pl.pallas_call(settle_kernel, in_specs=[smem()] + [vmem()] * 12, out_spec...  34.5 us
    pallas_call x1, Pallas kernels, encode(): pl.pallas_call(encode_kernel, grid=(pixels // tile,), in_specs=[smem(), s...  16.3 us
    unnamed x63, local copies, waits for them, and re-layouts  8.3 us

commit v1 on v0

--- a/solution.py
+++ b/solution.py
@@ -196,9 +196,47 @@
     return within, across
 
 
+class Relay:
+    def __init__(self, part, sems):
+        me = lax.axis_index("head")
+        self.me, self.near, self.across = me, (me + 1 - 2 * (me % 2), (me + 2) % 4), 3 - me
+        self.part, self.sems = part, sems
+
+    def copy(self, kind, target, slot, half):
+        return pltpu.make_async_remote_copy(
+            src_ref=self.part(slot, half),
+            dst_ref=self.part(slot, half),
+            send_sem=self.sems.at[0, kind, half],
+            recv_sem=self.sems.at[1, kind, half],
+            device_id={"head": target},
+        )
+
+    def start(self, halves=((0, 0), (1, 1), (0, 1), (1, 0))):
+        for side, half in halves:
+            self.copy(side, self.near[side], self.me, half).start()
+
+    def hand_on(self, side):
+        self.copy(side, self.near[side], self.near[side], side).wait_recv()
+        self.copy(2, self.near[1 - side], self.near[side], side).start()
+
+    def arrived(self, side):
+        self.copy(side, self.near[side], self.near[side], 1 - side).wait_recv()
+
+    def arrived_across(self):
+        for half in range(2):
+            self.copy(2, self.near[half], self.across, half).wait_recv()
+
+    def sent(self):
+        for half in range(2):
+            for side in range(2):
+                self.copy(side, self.near[side], self.me, half).wait_send()
+            self.copy(2, self.near[1 - half], self.near[half], half).wait_send()
+
+
 def encode_kernel(
-    place_ref, scale_ref, node_ref, prev_ref, target_ref, eps_ref, w_ref, in_ref, stat_ref, own_ref, all_ref,
-    pix, box, pair_box, sems, pair_sems
+    place_ref, scale_ref, node_ref, prev_ref, target_ref, eps_ref, w_ref,
+    in_ref, stat_ref, own_ref, all_ref,
+    pix, box, pair_box, sems, pair_sems,
 ):
     step = pl.program_id(0)
     rows = in_ref.shape[0]
@@ -328,12 +366,9 @@
     zero_ref[...] = h_zero
     normed, _ = standardize(h_zero)
     norm_ref[head] = (normed * (1 + mod_ref[0:1]) + mod_ref[1:2]).astype(bf16)
-    norms = Spread(
-        along("head"), lambda _: norm_ref.at[head], lambda i: norm_ref.at[i], head_sems.at[0], head_sems.at[1]
-    )
-    near = nearest_first(head, heads)
-    for other in near[:2]:
-        norms.copy(other, head).start()
+    half_rows = rows // 2
+    norms = Relay(lambda slot, half: norm_ref.at[slot, pl.ds(half * half_rows, half_rows)], head_sems)
+    norms.start()
 
     def halo(block):
         return [
@@ -385,17 +420,15 @@
     bands[...] = jnp.where(live, relative >> 8, -1).astype(f32).astype(bf16)
     spots[...] = (relative & 255).astype(f32).astype(bf16)
     each(steps // 4, count, 0)
-
-    norms.copy(near[0], near[0]).wait_recv()
-    for other in near[2:]:
-        norms.copy(other, head).start()
-    project(near[0])
-    norms.copy(near[1], near[1]).wait_recv()
-    project(near[1])
-    each(steps * 5 // 8, count, steps // 4)
-    for other in near[2:]:
-        norms.copy(other, other).wait_recv()
-        project(other)
+    norms.hand_on(0)
+    norms.hand_on(1)
+    each(steps * 3 // 8, count, steps // 4)
+    for side in range(2):
+        norms.arrived(side)
+        project(norms.near[side])
+    each(steps * 5 // 8, count, steps * 3 // 8)
+    norms.arrived_across()
+    project(norms.across)
     each(steps, count, steps * 5 // 8)
     each(steps, lambda step: count_out(step).wait(), steps - 2)
     stats.all("arrived")
@@ -406,7 +439,7 @@
             copy.wait()
 
     each(heads, finish, 0)
-    norms.all("sent")
+    norms.sent()
     stats.all("sent")
 
 
@@ -433,7 +466,7 @@
             pltpu.VMEM((NBR, heads * rows), bf16),
             pltpu.VMEM((NBR, heads * rows), bf16),
             pltpu.VMEM((2, depth, reach), bf16),
-            pltpu.SemaphoreType.DMA((2, heads)),
+            pltpu.SemaphoreType.DMA((2, 3, 2)),
             pltpu.SemaphoreType.DMA((2, groups)),
             pltpu.SemaphoreType.DMA((4, heads)),
             pltpu.SemaphoreType.DMA((2,)),
@@ -444,7 +477,7 @@
 
 
 def attend_kernel(
-    q_ref, kv_ref, count_ref, column_ref, ffn_ref, e_ref, mix_ref, out_ref, attn_all, ffn_all, s_scr, own, box, sems,
+    q_ref, kv_ref, count_ref, column_ref, ffn_ref, e_ref, mix_ref, out_ref, attn_out, ffn_out, s_scr, own, box, attn_all, ffn_all, sems,
     attn_sems, column_sems, ffn_sems, pair_sems, local_sems, chunk
 ):
     step = pl.program_id(0)
@@ -465,19 +498,16 @@
 
     within, across = pairs()
     place, pair = within[1], across[1]
-    attn_heads = Spread(
-        along("head"), lambda _: column_ref, lambda i: attn_all.at[i, :, place], attn_sems.at[0], attn_sems.at[1]
-    )
     ffn_pairs = Spread(
         across, lambda _: ffn_ref, lambda i: ffn_all.at[head, i, place], column_sems.at[0], column_sems.at[1]
     )
-    ffn_heads = Spread(
-        along("head"),
-        lambda _: ffn_all.at[head, :, place],
-        lambda i: ffn_all.at[i, :, place],
-        ffn_sems.at[0],
-        ffn_sems.at[1],
-    )
+    count = across[0]
+
+    def half_of(array):
+        return lambda slot, half: array.at[slot, pl.ds(half * (count // 2), count // 2), place]
+
+    attn_heads = Relay(half_of(attn_all), attn_sems)
+    ffn_heads = Relay(half_of(ffn_all), ffn_sems)
     stay = [
         pltpu.make_async_copy(column_ref, attn_all.at[head, :, place], local_sems.at[0]),
         pltpu.make_async_copy(ffn_ref, ffn_all.at[head, pair, place], local_sems.at[1]),
@@ -495,23 +525,35 @@
 
     @pl.when(step == 0)
     def _():
+        for copy in stay:
+            copy.start()
         meet(["head", "node"])
         ffn_pairs.all("start")
-        attn_heads.all("start")
-        for copy in stay:
-            copy.start()
-
-    @pl.when(step == steps * 5 // 16)
-    def _():
-        ffn_pairs.all("arrived")
         for copy in stay:
             copy.wait()
-        ffn_heads.all("start")
-
-    @pl.when(step == steps * 14 // 16)
-    def _():
-        attn_heads.all("arrived")
-        ffn_heads.all("arrived")
+        attn_heads.start()
+
+    @pl.when(step == 5)
+    def _():
+        attn_heads.hand_on(0)
+        attn_heads.hand_on(1)
+
+    @pl.when(step == 5)
+    def _():
+        ffn_pairs.all("arrived")
+        ffn_heads.start()
+
+    @pl.when(step == 12)
+    def _():
+        ffn_heads.hand_on(0)
+        ffn_heads.hand_on(1)
+
+    @pl.when(step == 15)
+    def _():
+        for heads_of in (attn_heads, ffn_heads):
+            for side in range(2):
+                heads_of.arrived(side)
+            heads_of.arrived_across()
 
         def begin(h):
             for which in range(2):
@@ -577,8 +619,17 @@
                 swap(h, which, 1 - place).wait_recv()
 
         each(heads, end, 0)
-        for spread in (attn_heads, ffn_pairs, ffn_heads):
-            spread.all("sent")
+        outs = [
+            pltpu.make_async_copy(attn_all, attn_out, local_sems.at[0]),
+            pltpu.make_async_copy(ffn_all, ffn_out, local_sems.at[1]),
+        ]
+        for put in outs:
+            put.start()
+        for put in outs:
+            put.wait()
+        ffn_pairs.all("sent")
+        attn_heads.sent()
+        ffn_heads.sent()
 
 
 def attend(query, keyval, counts, column, ffn_share, heads, tile, chunk):
@@ -603,10 +654,12 @@
             pltpu.VMEM((tile, reach), f32),
             pltpu.VMEM((heads, rows, HD), bf16),
             pltpu.VMEM((heads, rows, HD), bf16),
+            pltpu.VMEM((heads, count, 2, *column.shape[1:]), bf16),
+            pltpu.VMEM((heads, count, 2, *ffn_share.shape), bf16),
             dma(2, heads, rows // tile),
-            dma(2, heads),
+            dma(2, 3, 2),
             dma(2, count),
-            dma(2, heads),
+            dma(2, 3, 2),
             dma(2, 2, heads),
             dma(2),
         ],
@@ -853,7 +906,7 @@
 
 
 def middle_kernel(
-    place_ref, scale_ref, mixed_ref, zero_ref, wa_ref, wf_ref, mod_ref, wdec_ref, weight_ref,
+    place_ref, scale_ref, mixed_ref, zero_ref, wa_ref, wf_ref, mod_ref, wdec_ref, stat_ref,
     node_ref, read_ref, target_ref, eps_ref,
     done_ref, dmix_ref, pair_ref, gdec_ref, gmod_ref, loss_ref,
     one_scr, two_scr, norm_scr, up_scr, act_scr, dec_box, hits, turned, total,
@@ -872,15 +925,7 @@
     pixel_end = node_tiles + pixel_tiles
     others = nearest_first(head, heads)
 
-    def dec_copy(other, slot, t):
-        cols = pl.ds(t * tile, tile)
-        return pltpu.make_async_remote_copy(
-            src_ref=dec_box.at[head, :, cols],
-            dst_ref=dec_box.at[slot, :, cols],
-            send_sem=dec_sems.at[0, other, t],
-            recv_sem=dec_sems.at[1, slot, t],
-            device_id={"head": other},
-        )
+    decs = Relay(lambda slot, half: dec_box.at[slot, :, pl.ds(half * tile, tile)], dec_sems)
 
     d_spread = Spread(along("head"), lambda o: d_own.at[o], lambda i: d_box.at[i], d_sems.at[0], d_sems.at[1])
 
@@ -942,8 +987,9 @@
             high, low = halves(contract(wdec_ref[...], final, 1, 1))
             dec_box[head, :SLIM, lines] = high
             dec_box[head, SLIM:, lines] = low
-            for other in others:
-                dec_copy(other, head, t).start()
+            decs.start(((0, t), (1, t)))
+            if t == 1:
+                decs.hand_on(0)
 
     @pl.when((step >= node_tiles) & (step < pixel_end))
     def _():
@@ -956,9 +1002,10 @@
 
         @pl.when(step == node_tiles)
         def _():
-            for other in others:
-                for t in range(node_tiles):
-                    dec_copy(other, other, t).wait_recv()
+            decs.hand_on(1)
+            for side in range(2):
+                decs.arrived(side)
+            decs.arrived_across()
 
         field = sum(contract(dec_box[h], hits[h * rows : (h + 1) * rows], 1, 0) for h in range(heads))
         field = (field[:VARS] + field[SLIM : SLIM + VARS]) / 3.0
@@ -966,9 +1013,10 @@
         noisy = target + scale_ref[0] * eps_ref[...]
         error = scale_ref[2] * noisy + scale_ref[3] * field - target
         valid = (node_ref[...] - place_ref[0] < place_ref[2]).astype(f32)
-        weighted = valid * weight_ref[:, 0:1]
+        valid_pixels = stat_ref[SLIM - 1 : SLIM, 0:1]
+        weighted = valid * (scale_ref[4] / (stat_ref[:VARS, 0:1] / valid_pixels + norm_eps))
         loss_ref[:VARS] += fold_lanes(weighted * error * error)
-        high, low = halves(scale_ref[4] * weighted * error)
+        high, low = halves(scale_ref[3] * (2.0 / (valid_pixels * VARS)) / 3.0 * weighted * error)
         turned[:VARS] = high
         turned[SLOT : SLOT + VARS] = low
         total[...] += contract(hits[...], turned[...], 1, 1)
@@ -1047,14 +1095,14 @@
                 for other in others:
                     d_spread.copy(other, head).wait_send()
                     for u in range(node_tiles):
-                        dec_copy(other, head, u).wait_send()
                         dmix_copy(other, head, u).wait_send()
+                decs.sent()
                 for h in range(heads):
                     for part in range(2):
                         pair_copy(h, part).wait_send()
 
 
-def middle(place, scales, mixed, h_zero, w_attn, w_ffn, modulation, w_dec, weight, node_row, read_rows, target, eps, groups):
+def middle(place, scales, mixed, h_zero, w_attn, w_ffn, modulation, w_dec, stat, node_row, read_rows, target, eps, groups):
     heads, rows, _ = mixed.shape
     width = h_zero.shape[1]
     node_tiles, pixels = 2, target.shape[1] // heads
@@ -1109,7 +1157,7 @@
             full(heads, width, grads),
             low(2, *pair),
             low(*pair),
-            dma(2, heads, node_tiles),
+            dma(2, 3, 2),
             dma(2, heads),
             dma(2, heads, node_tiles),
             dma(2, 2, heads),
@@ -1118,7 +1166,7 @@
         compiler_params=remote(62, 7),
         name="middle",
     )(
-        place, scales, mixed, h_zero, w_attn, w_ffn, modulation, w_dec, weight, node_row, read_rows, target, eps
+        place, scales, mixed, h_zero, w_attn, w_ffn, modulation, w_dec, stat, node_row, read_rows, target, eps
     )
 
 
@@ -1127,7 +1175,7 @@
     small_ref, share_ref, full_ref, sums_ref,
     q_low, q_pair, q_sum, q_box, q_share, q_full,
     parts, part_box, part_sum, part_own, pay, heard, tally, tallies,
-    pair_sems, q_sems, f_sems, a_sems, n_sems, b_sems, t_sems,
+    pair_sems, q_sems, f_sems, a_sems, n_sems, b_sems, t_sems, s_sems,
 ):
     heads, width = w_ref.shape[0], w_ref.shape[1]
     share_rows = share_ref.shape[0]
@@ -1227,7 +1275,11 @@
     tell.all("start")
     tallies[head] = tally[...]
     for t in range(groups):
-        small_ref[8 * t : 8 * t + 8] = heard[t, :, :width]
+        small_ref[head, 8 * t : 8 * t + 8] = heard[t, :, :width]
+    smalls = Spread(
+        along("head"), lambda _: small_ref.at[head], lambda i: small_ref.at[i], s_sems.at[0], s_sems.at[1]
+    )
+    smalls.all("start")
     tell.all("arrived")
     sums_ref[...] = sum(tallies[h] for h in range(heads))
 
@@ -1236,7 +1288,8 @@
     for c in range(2):
         for z in range(count):
             full_ref[2 * z + c] = q_full[c, z]
-    for spread in (q_over, over_heads, f_over, over_nodes, back, tell):
+    smalls.all("arrived")
+    for spread in (q_over, over_heads, f_over, over_nodes, back, tell, smalls):
         spread.all("sent")
 
 
@@ -1253,7 +1306,7 @@
         in_specs=[smem()] + [vmem()] * 12,
         out_specs=[vmem()] * 4,
         out_shape=[
-            jax.ShapeDtypeStruct((8 * groups, width), f32),
+            jax.ShapeDtypeStruct((heads, 8 * groups, width), f32),
             jax.ShapeDtypeStruct(share, f32),
             jax.ShapeDtypeStruct((groups, *share), bf16),
             jax.ShapeDtypeStruct((8, 128), f32),
@@ -1279,6 +1332,7 @@
             dma(2, heads),
             dma(2, groups),
             dma(2, groups),
+            dma(2, heads),
             dma(2, heads),
         ],
         compiler_params=remote(56, 1),
@@ -1321,26 +1375,48 @@
     return pivots
 
 
-def renew_kernel(gram_ref, product_ref, small_ref, out_ref, all_ref, gram, both, work, done, box, sems):
-    count, size = gram_ref.shape[:2]
+def finish_kernel(
+    sums_ref, small_ref, qkv_share_ref, big_share_ref, qkv_ref, big_ref, stats_ref, basis_ref,
+    layer_ref, first_ref, second_ref, feat_ref,
+    enc_ref, enc1_ref, enc2_ref, cond_ref, cond1_ref, cond2_ref, dec_ref, dec1_ref, dec2_ref,
+    out_ref, stats_out, layer_out, first_out, second_out,
+    enc_out, enc1_out, enc2_out, cond_out, cond1_out, cond2_out, dec_out, dec1_out, dec2_out,
+    gram, both, work, done, shares,
+):
+    count, size = stats_ref.shape[:2]
     k = pl.program_id(0)
-
-    head = lax.axis_index("head")
-    smalls = Spread(along("head"), lambda _: small_ref, lambda i: box.at[i], sems.at[0], sems.at[1])
+    clip = clip_limit / jnp.maximum(jnp.sqrt(sums_ref[0:1, 0:1]), clip_limit)
 
     @pl.when(k == 0)
     def _():
-        gram[...] = gram_ref[...]
-        both[...] = product_ref[...]
-        meet(["head"])
-        smalls.all("start")
-        box[head] = small_ref[...]
-
-    @pl.when(k == pl.num_programs(0) - 1)
-    def _():
-        smalls.all("arrived")
-        all_ref[...] = box[...]
-        smalls.all("sent")
+        cuts = [slice(0, size), slice(size, 2 * size), slice(2 * size, 3 * size)]
+        shares[0] = jnp.concatenate([qkv_share_ref[...], big_share_ref[:, cuts[2].start :]], 1)
+        grads = [jnp.concatenate([qkv_ref[...], big_ref[:, cuts[2].start :]], 1)]
+        for m in (1, 2):
+            shares[m] = big_share_ref[:, cuts[m - 1]]
+            grads.append(big_ref[:, cuts[m - 1]])
+        for m in range(count):
+            raw = contract(grads[m], grads[m], 0, 0)
+            new = beta_stats * stats_ref[m] + (1 - beta_stats) * (clip * (clip * raw))
+            stats_out[m] = new
+            product = contract(new, basis_ref[m], 1, 0, highest)
+            both[m] = product
+            gram[m] = contract(product, product, 0, 0, highest)
+
+    i = jnp.minimum(k, count - 1)
+    rotated = contract(clip * shares[i], basis_ref[i], 1, 0, highest)
+    first_new = beta_first * first_ref[i] + (1 - beta_first) * rotated
+    second_new = beta_second * second_ref[i] + (1 - beta_second) * rotated * rotated
+    first_out[i] = first_new
+    second_out[i] = second_new
+    direction = (
+        first_new
+        / (1 - beta_first**STEP)
+        / (jnp.sqrt(second_new / (1 - beta_second**STEP)) + adam_epsilon)
+    )
+    layer_out[i] = layer_ref[i] - rate_layer * (
+        contract(direction, basis_ref[i], 1, 1, highest) + decay_rate * layer_ref[i]
+    )
 
     at = pl.ds(pl.multiple_of(k * BLOCK, BLOCK), BLOCK)
     unit = lax.broadcasted_iota(jnp.int32, (BLOCK, BLOCK), 0) == lax.broadcasted_iota(
@@ -1363,27 +1439,49 @@
                     both[m, :, rest:] -= contract(panel, left, 1, 1, highest)
                     gram[m, rest:, rest:] -= contract(left, left, 1, 1, highest)
 
-
-def renew(gram, product, small, heads):
-    count, size = gram.shape[:2]
-    gathered = (heads, *small.shape)
+    @pl.when(k == pl.num_programs(0) - 1)
+    def _():
+        flat = clip * small_ref[...]
+
+        def adam(grad, cols, refs, outs):
+            for out, new in zip(outs, adam_small(refs[0][:, cols], grad, refs[1][:, cols], refs[2][:, cols])):
+                out[:, cols] = new
+
+        every = slice(None)
+        adam(flat[: 2 * VARS], every, (enc_ref, enc1_ref, enc2_ref), (enc_out, enc1_out, enc2_out))
+        adam(flat[2 * VARS : 3 * VARS], every, (dec_ref, dec1_ref, dec2_ref), (dec_out, dec1_out, dec2_out))
+        width = flat.shape[1]
+        for j in range(4):
+            grad = feat_ref[:, 0:1] * flat[3 * VARS + j : 3 * VARS + j + 1]
+            adam(
+                grad,
+                slice(j * width, (j + 1) * width),
+                (cond_ref, cond1_ref, cond2_ref),
+                (cond_out, cond1_out, cond2_out),
+            )
+
+
+def finish(sums, small, qkv_share, big_share, qkv_full, big_full, stats, basis, layers, feat, enc, cond, dec):
+    count, size = stats.shape[:2]
+    inputs = (sums, small, qkv_share, big_share, qkv_full, big_full, stats, basis, *layers, feat, *enc, *cond, *dec)
+    like = lambda x: jax.ShapeDtypeStruct(x.shape, f32)
+    outs = [stats, *layers, *enc, *cond, *dec]
     return pl.pallas_call(
-        renew_kernel,
+        finish_kernel,
         grid=(size // BLOCK,),
-        in_specs=[whole(gram.shape), whole(gram.shape), whole(small.shape)],
-        out_specs=[pl.BlockSpec((count, size, BLOCK), lambda k: (0, 0, k)), whole(gathered)],
-        out_shape=[jax.ShapeDtypeStruct(gram.shape, f32), jax.ShapeDtypeStruct(gathered, f32)],
+        in_specs=[whole(x.shape) for x in inputs],
+        out_specs=[pl.BlockSpec((count, size, BLOCK), lambda k: (0, 0, k))] + [whole(x.shape) for x in outs],
+        out_shape=[like(stats)] + [like(x) for x in outs],
         scratch_shapes=[
             pltpu.VMEM((count, size, size), f32),
             pltpu.VMEM((count, size, size), f32),
             pltpu.VMEM((count, BLOCK, 2 * BLOCK), f32),
             pltpu.VMEM((count, BLOCK, BLOCK), f32),
-            pltpu.VMEM(gathered, f32),
-            pltpu.SemaphoreType.DMA((2, heads)),
+            pltpu.VMEM(layers[0].shape, f32),
         ],
-        compiler_params=remote(48, 6),
-        name="renew",
-    )(gram, product, small)
+        compiler_params=params(60),
+        name="finish",
+    )(*inputs)
 
 
 def local(
@@ -1435,7 +1533,8 @@
     read_rows = pix_read.T
     place = jnp.stack([block_start, quarter * rows, valid_count[0], quarter]).astype(jnp.int32)
     node_in, stat, column, w_attn = encode(
-        place, jnp.stack([noise_sigma, input_scale]), node_row, prev_t, target_t, eps_t, low_w[0], rows, 1024, groups
+        place, jnp.stack([noise_sigma, input_scale]), node_row, prev_t, target_t, eps_t, low_w[0],
+        rows, 1024, groups
     )
     w_attn = w_attn.reshape(width, -1)
 
@@ -1447,21 +1546,15 @@
     )
     norm_all, query = norm_all.reshape(nodes, -1), query.reshape(nodes, -1)
     keyval = keyval.reshape(3, nodes, -1)
-    stat_sum = stat[:, 0]
-    count_sum = stat_sum[SLIM - 1]
-    var_weight = 1.0 / (stat_sum[:VARS] / count_sum + norm_eps)
-    loss_count = count_sum * VARS
+    loss_count = stat[SLIM - 1, 0] * VARS
     e, mix, mixed, attn_all, ffn_all = attend(query, keyval, counts, column, ffn_share, heads, 128, 512)
     attn_all = attn_all.reshape(heads, width, -1)
     ffn_all = ffn_all.reshape(heads, width, -1)
 
     w_dec_t = jnp.zeros((SLIM, width), bf16).at[:VARS].set(w_dec.T.astype(bf16))
-    scales = jnp.stack(
-        [noise_sigma, input_scale, skip_scale, output_scale, output_scale * (2.0 / loss_count) / 3.0]
-    )
-    weight = jnp.broadcast_to((loss_scale * var_weight)[:, None], (VARS, 128))
+    scales = jnp.stack([noise_sigma, input_scale, skip_scale, output_scale, loss_scale])
     d_one, d_mixed, pair_sum, grad_dec, gmod_two, loss_part = middle(
-        place, scales, mixed, h_zero, attn_all, ffn_all, modulation, w_dec_t, weight, node_row, read_rows,
+        place, scales, mixed, h_zero, attn_all, ffn_all, modulation, w_dec_t, stat, node_row, read_rows,
         target_t, eps_t, groups,
     )
     d_mixed = d_mixed.reshape(nodes, HD)
@@ -1473,61 +1566,32 @@
         feat_sq, dq, dkv, attn_all, h_zero, d_one, node_in, modulation, grad_dec, gmod_two, grad_qkv, big_share,
         loss_part, groups,
     )
-    big_full = big_full.reshape(width, -1)
-    layer_share = jnp.stack(
-        [
-            jnp.concatenate([qkv_share, big_share[:, 2 * width :]], 1),
-            big_share[:, :width],
-            big_share[:, width : 2 * width],
-        ]
-    )
-    grad_norm = jnp.sqrt(sums[0, 0])
-    loss_sum = sums[1, 0]
-    clip_factor = clip_limit / jnp.maximum(grad_norm, clip_limit)
-    clipped = clip_factor * layer_share
-    grad_full = jnp.stack(
-        [
-            jnp.concatenate([qkv_full.reshape(width, -1), big_full[:, 2 * width :]], 1),
-            big_full[:, :width],
-            big_full[:, width : 2 * width],
-        ]
-    )
-    raw_stat = jnp.einsum("idb,idc->ibc", grad_full, grad_full, preferred_element_type=f32)
-    stat_new = clip_factor * (clip_factor * raw_stat)
-    basis_old = soap_basis[:, 0]
-    rotated = jnp.einsum("idb,ibc->idc", clipped, basis_old, precision=highest)
-    first_new = beta_first * soap_first + (1 - beta_first) * rotated
-    second_new = beta_second * soap_second + (1 - beta_second) * rotated * rotated
-    direction = (
-        first_new
-        / (1 - beta_first**STEP)
-        / (jnp.sqrt(second_new / (1 - beta_second**STEP)) + adam_epsilon)
-    )
-    step_back = jnp.einsum("idc,ibc->idb", direction, basis_old, precision=highest)
-    layer_new = layer_w - rate_layer * (step_back + decay_rate * layer_w)
-    stats_new = beta_stats * soap_stats[:, 0] + (1 - beta_stats) * stat_new
-    product = jnp.einsum("ibc,icd->ibd", stats_new, basis_old, precision=highest)
-    gram_matrix = jnp.einsum("ibc,ibd->icd", product, product, precision=highest)
-    basis_new, small = renew(gram_matrix, product, small, heads)
-    small = small.reshape(-1, width)
-    grad_enc = small[: 2 * VARS]
-    grad_dec = small[2 * VARS : 3 * VARS]
-    grad_cond = noise_feat[:, None] * small[3 * VARS : 3 * VARS + 4].reshape(1, -1)
-    enc_new = adam_small(w_enc, clip_factor * grad_enc, enc_first, enc_second)
-    cond_new = adam_small(w_cond, clip_factor * grad_cond, cond_first, cond_second)
-    dec_new = adam_small(w_dec.T, clip_factor * grad_dec, dec_first.T, dec_second.T)
+    basis_new, stats_new, layer_new, first_new, second_new, *small_new = finish(
+        sums,
+        small.reshape(-1, width),
+        qkv_share,
+        big_share,
+        qkv_full.reshape(width, -1),
+        big_full.reshape(width, -1),
+        soap_stats[:, 0],
+        soap_basis[:, 0],
+        (layer_w, soap_first, soap_second),
+        jnp.broadcast_to(noise_feat[:, None], (NF, 128)),
+        (w_enc, enc_first, enc_second),
+        (w_cond, cond_first, cond_second),
+        (w_dec.T, dec_first.T, dec_second.T),
+    )
     return (
-        jnp.reshape(loss_sum, (1,)),
+        jnp.reshape(sums[1, 0], (1,)),
         jnp.reshape(loss_count, (1,)),
-        jnp.reshape(grad_norm, (1,)),
+        jnp.reshape(jnp.sqrt(sums[0, 0]), (1,)),
         layer_new,
         first_new,
         second_new,
         basis_new[:, None],
         stats_new[:, None],
-        *enc_new,
-        *cond_new,
-        *(x.T for x in dec_new),
+        *small_new[:6],
+        *(x.T for x in small_new[6:]),
     )
 
 

time: 387 us -> 368 us (0.951)
  matrix products: 19.6 us -> 0.24 us
  Pallas kernels: 333 us -> 341 us
  other arithmetic: 7.73 us -> 2.6 us
    pallas_call x1, Pallas kernels: 40 us -> 59.9 us  [finish(): pl.pallas_call(finish_kernel, grid=(size // BLOCK,), in_specs=[whole(x.sh...]
    dot_general x5 -> x0, matrix products: 19.4 us -> none  [the longest x1 6.87 us: local(): jnp.einsum('ibc,ibd->icd', product, product, precision=highest)]
    pallas_call x1, Pallas kernels: 73.4 us -> 61.3 us  [middle(): pl.pallas_call(functools.partial(middle_kernel, node_tiles=node_tiles, pi...]
    pallas_call x1, Pallas kernels: 34.5 us -> 39.8 us  [settle(): pl.pallas_call(settle_kernel, in_specs=[smem()] + [vmem()] * 12, out_spec...]
    unnamed x63 -> x20, local copies, waits for them, and re-layouts: 8.3 us -> 5.93 us
where the time goes in v1:
time: 368 us; the launch traced here: 361 us
  Pallas kernels  341 us (93%)
  local copies, waits for them, and re-layouts  11.7 us (3%)
  between operations  6.09 us (2%)
    pallas_call x1, Pallas kernels, attend_back(): pl.pallas_call(functools.partial(attend_back_kernel, chunk=chunk), grid=(...  73.6 us
    pallas_call x1, Pallas kernels, middle(): pl.pallas_call(functools.partial(middle_kernel, node_tiles=node_tiles, pi...  61.3 us
    pallas_call x1, Pallas kernels, finish(): pl.pallas_call(finish_kernel, grid=(size // BLOCK,), in_specs=[whole(x.sh...  59.9 us
    pallas_call x1, Pallas kernels, attend(): pl.pallas_call(functools.partial(attend_kernel, chunk=chunk), grid=(nodes...  50.4 us
    pallas_call x1, Pallas kernels, settle(): pl.pallas_call(settle_kernel, in_specs=[smem()] + [vmem()] * 12, out_spec...  39.8 us
    pallas_call x1, Pallas kernels, open_nodes(): pl.pallas_call(open_kernel, in_specs=[vmem()] * 7, out_specs=[vmem()] * 5...  39.4 us
    pallas_call x1, Pallas kernels, encode(): pl.pallas_call(encode_kernel, grid=(pixels // tile,), in_specs=[smem(), s...  16.2 us

profile of v1, /device:TPU:0, one launch (start us, length us, event | category | flops | bytes accessed | tf_op | source)
XLA Modules:
  0.0 361.2 jit_solution(14458663026704046121)
XLA Ops:
  1.4 0.7 multiply_reduce_fusion
  3.0 1.0 convert_element_type.18
  4.0 2.2 copy-done
  6.2 0.8 copy-done.4
  7.0 16.2 %encode.1 = (f32[512,256]{1,0:T(8,128)S(1)}, f32[96,128]{1,0:T(8,128)S(1)}, bf16[4,64,512]{2,1,0:T(8,128)(2,1)S(1)}, bf16[4,2,64,512]{3,2,1,0:T(8,128)(2,1)S(1)}) custom-call(s32[4]{0:T(128)S(1)} %pad_add_fusion.place_ref, f32[2]{0:T(128)S(1)} %pad_maximum_fusion.2.scale_ref, s32[1,12288]{1,0:T(1,128)S(1)} %bitcast.66, f32[84,12288]{1,0:T(8,128)S(1)} %bitcast.63, ...), custom_call_target="tpu_custom_call" | custom-call | tf_op jit(solution)/shard_map/encode/pallas_call | solution.py:298
  23.3 0.8 copy-done.1
  24.1 0.8 copy-done.2
  24.9 0.7 copy-done.3
  25.6 0.6 copy-done.5
  26.3 0.7 scatter.6
  27.0 0.2 fusion
  27.2 0.6 copy.52
  27.8 39.4 %open_nodes.1 = (f32[512,512]{1,0:T(8,128)}, bf16[4,512,512]{2,1,0:T(8,128)(2,1)}, bf16[4,512,128]{2,1,0:T(8,128)(2,1)}, bf16[3,4,512,256]{3,2,1,0:T(8,128)(2,1)...) custom-call(f32[512,256]{1,0:T(8,128)} %copy-done.1, bf16[256,512]{1,0:T(8,128)(2,1)} %bitcast.83, f32[4,512]{1,0:T(4,128)} %bitcast.91, ...), custom_call_target="tpu_custom_call" | custom-call | tf_op jit(solution)/shard_map/open_nodes/pallas_call | solution.py:451
  67.3 0.6 stack.42.scale_ref
  67.9 0.7 pad_maximum_fusion.ffn_ref
  68.6 50.4 %attend.1 = (bf16[2048,6144]{1,0:T(8,128)(2,1)}, f32[2048,256]{1,0:T(8,128)}, bf16[4,512,128]{2,1,0:T(8,128)(2,1)}, bf16[4,4,2,64,512]{4,3,2,1,0:T(8,128)(2,1)}, bf16[4,4,2,64,1024]{4,3,2,1,0:T(8,128)(2,1)}) custom-call(bf16[2048,128]{1,0:T(8,128)(2,1)} %bitcast.78, bf16[3,2048,256]{2,1,0:T(8,128)(2,1)} %bitcast.71, ...), custom_call_target="tpu_custom_call" | custom-call | tf_op jit(solution)/shard_map/attend/pallas_call | solution.py:641
  119.0 0.7 scatter.9.wdec_ref
  119.6 61.3 %middle.1 = (f32[512,512]{1,0:T(8,128)}, bf16[4,512,128]{2,1,0:T(8,128)(2,1)}, bf16[4,4,64,1152]{3,2,1,0:T(8,128)(2,1)}, f32[96,512]{1,0:T(8,128)}, f32[8,512]{1,0:T(8,128)}, /*index=5*/f32[96,128]{1,0:T(8,128)}) custom-call(s32[4]{0:T(128)} %copy-done.6, f32[5]{0:T(128)} %stack.42.scale_ref, bf16[4,512,128]{2,1,0:T(8,128)(2,1)} %get-tuple-element.92.mixed_ref, ...), custom_call_target="tpu_custom_call" | custom-call | tf_op jit(solution)/shard_map/middle/pallas_call | solution.py:1123
  180.9 73.6 %attend_back.1 = (bf16[4,512,128]{2,1,0:T(8,128)(2,1)}, bf16[4,256,512]{2,1,0:T(8,128)(2,1)}, f32[512,384]{1,0:T(8,128)}, f32[64,1152]{1,0:T(8,128)}, bf16[4,2,64,1152]{3,2,1,0:T(8,128)(2,1)}) custom-call(bf16[2048,128]{1,0:T(8,128)(2,1)} %bitcast.79, bf16[2048,128]{1,0:T(8,128)(2,1)} %bitcast.85, f32[2048,256]{1,0:T(8,128)} %get-tuple-element.98.mix_ref, ...), custom_call_target="tpu_custom_call" | custom-call | tf_op jit(solution)/shard_map/attend_back/pallas_call | solution.py:858
  254.5 39.8 %settle.1 = (f32[4,64,512]{2,1,0:T(8,128)}, f32[64,384]{1,0:T(8,128)}, bf16[8,64,384]{2,1,0:T(8,128)(2,1)}, f32[8,128]{1,0:T(8,128)}) custom-call(f32[1]{0:T(128)} %bitcast.1.feat_ref, bf16[4,512,128]{2,1,0:T(8,128)(2,1)} %get-tuple-element.102.dq_ref, bf16[4,256,512]{2,1,0:T(8,128)(2,1)} %get-tuple-element.103.dkv_ref, bf16[4,512,512]{2,1,0:T(8,128)(2,1)} %bitcast.74, ...), custom_call_target="tpu_custom_call" | custom-call | tf_op jit(solution)/shard_map/settle/pallas_call | solution.py:1304
  294.4 1.3 fusion.6
  295.6 1.2 slice.59
  298.2 0.7 broadcast_in_dim.6.feat_ref
  298.8 59.9 %finish.1 = (f32[3,512,512]{2,1,0:T(8,128)}, f32[3,512,512]{2,1,0:T(8,128)}, f32[3,64,512]{2,1,0:T(8,128)}, f32[3,64,512]{2,1,0:T(8,128)}, f32[3,64,512]{2,1,0:T...) custom-call(f32[8,128]{1,0:T(8,128)} %get-tuple-element.110.sums_ref, ...), custom_call_target="tpu_custom_call" | custom-call | tf_op jit(solution)/shard_map/finish/pallas_call | solution.py:1469
  (21 shorter events, 0.3 us)
Async XLA Ops:
  2.8 20.4 %copy-start.6 = (s32[4]{0:T(128)}, s32[4]{0:T(128)S(1)}, u32[]{:S(2)}) copy-start(s32[4]{0:T(128)S(1)} %pad_add_fusion.place_ref) | copy-start | bytes 52
  4.0 2.2 copy-start
  6.2 0.8 copy-start.4
  7.0 19.1 %copy-start.7 = (f32[168,512]{1,0:T(8,128)S(1)}, f32[168,512]{1,0:T(8,128)}, u32[]{:S(2)}) copy-start(f32[168,512]{1,0:T(8,128)} %enc_ref.1) | copy-start | bytes 1032196
  7.0 19.9 %copy-start.8 = (f32[32,2048]{1,0:T(8,128)S(1)}, f32[32,2048]{1,0:T(8,128)}, u32[]{:S(2)}) copy-start(f32[32,2048]{1,0:T(8,128)} %cond_ref.1) | copy-start | bytes 786436
  23.3 0.8 copy-start.1
  24.1 0.8 copy-start.2
  24.9 0.7 copy-start.3
  25.6 0.6 copy-start.5
  68.6 50.4 %copy-start.9 = (f32[512,84]{0,1:T(8,128)S(1)}, f32[512,84]{0,1:T(8,128)}, u32[]{:S(2)}) copy-start(f32[512,84]{0,1:T(8,128)} %param.38) | copy-start | bytes 516100
